TPU v7x, 32 devices: a whole 2x2x4 slice. The times are simulated.
32 devices in a mesh: users: 16 (over z, y, core), items: 2 (over x).
Axes of the slice: x: 2, y: 2, z: 4, core: 2. Of those that a mesh axis runs over, the one named last changes fastest.
Arguments:
- interactions: bfloat16 [3, 20480, 512], P(None, 'users', 'items')
- matchings: int32 [3], replicated, may hold values from 1 to 15, as said below
- user_shape: bfloat16 [20480, 128], P('users'), may hold values from 0.5 to 2
- item_shape: bfloat16 [8192, 128], P(('users', 'items')), may hold values from 0.5 to 2
Outputs:
- user_log: bfloat16 [20480, 128], P('users')
- item_log: bfloat16 [8192, 128], P(('users', 'items'))
Inputs may be any that keep to these rules, and one draw needn't show every extreme that they name: matchings[0] and matchings[1] are two different values of 1 to 14, and the last matching is 15.
All inputs are finite; a program needn't handle non-finite values.
Results may differ from a plain program's by a relative error of at most 0.0012.
The roundings to bfloat16 on the way count: a program that leaves them out, or rounds other values in their place, can miss the bound.
Values sent between devices are 32-bit elements; how exact they have to be, the bound alone decides.
No kernel may reach another device: no remote copies, remote signals or barrier semaphores. Data moves between devices by JAX's collectives and lax.ppermute only.
A program may use at most 64 MiB of HBM per device.

v0:
```python
import functools

import jax
import jax.numpy as jnp
from jax import lax
from jax.experimental import pallas as pl
from jax.experimental.pallas import tpu as pltpu
from jax.sharding import PartitionSpec as P

STRATA = 3
TILE = 64
START_TILE = 128
REDO_TILE = 32
F32 = jnp.float32
BF16 = jnp.bfloat16


def chunk_rows(rows):
    first = max(rows * 3 // 10 // START_TILE, 1) * START_TILE
    return [first, rows - first] if first < rows else [rows]


def last_cuts(rows):
    count = -(-rows // (4 * TILE))
    tiles_of = [rows // TILE // count + (i < rows // TILE % count) for i in range(count)]
    return [n * TILE for n in tiles_of] if rows % TILE == 0 else [rows]


def psi_parts(x):
    small = x < 8.0
    w = jnp.where(small, x + 3.5, x - 0.5)
    q = x * (x + 3.0)
    q2 = q + 2.0
    bounded = jnp.minimum(w, 1e9)
    square = bounded * bounded
    steps = jnp.where(small, q * q2, 1.0)
    r = 1.0 / (square * steps)
    s = r * steps
    shift = (2.0 * x + 3.0) * (q + q2) * (r * square)
    g = s * (1.0 / 24.0 - s * (7.0 / 960.0 - s * (31.0 / 8064.0 - s * (127.0 / 30720.0))))
    return w, g - jnp.where(small, shift, 0.0)


def psi_any(x):
    mirrored = x < 0.5
    w, g = psi_parts(jnp.where(mirrored, 1.0 - x, x))
    value = jnp.log(w) + g
    t = x - jnp.floor(x + 0.5)
    u = 3.14159265358979 * t
    v = u * u
    sin = 1.0 / 6227020800.0
    for c in (-1.0 / 39916800.0, 1.0 / 362880.0, -1.0 / 5040.0, 1.0 / 120.0, -1.0 / 6.0, 1.0):
        sin = sin * v + c
    cos = -1.0 / 87178291200.0
    for c in (1.0 / 479001600.0, -1.0 / 3628800.0, 1.0 / 40320.0, -1.0 / 720.0, 1.0 / 24.0, -0.5, 1.0):
        cos = cos * v + c
    value = jnp.where(mirrored, value - 3.14159265358979 * cos / (sin * u), value)
    return jnp.where((x <= 0.0) & (x == jnp.floor(x)), jnp.nan, value)


LOWEST = 0.01
HIGHEST = 1e30


def usual(rte):
    return jnp.where(rte <= HIGHEST, rte, -1.0)


def above(low):
    return jnp.min(low) >= LOWEST


def folded(x):
    return x.reshape(x.shape[0] // 8, 8, x.shape[1])


def tiles(rows):
    step = TILE if rows % TILE == 0 else rows
    return [(at, step) for at in range(0, rows, step)]


def redo_loop(rows, step, carry=None):
    size = REDO_TILE if rows % REDO_TILE == 0 else 8
    return lax.fori_loop(
        0, rows // size, lambda i, c: step(pl.multiple_of(i * size, size), size, c), carry)


def exp_tile(x, rte, general):
    shape = x.shape
    x = folded(x)
    if general:
        value = psi_any(x)
        if rte is not None:
            value = value - jnp.log(rte)[None]
        value = jnp.exp(value)
    else:
        w, g = psi_parts(x)
        value = w if rte is None else w * (1.0 / rte)[None]
        value = value * jnp.exp(g)
    mean = x if rte is None else x / rte[None] if general else x * (1.0 / rte)[None]
    return value.reshape(shape).astype(BF16), jnp.sum(mean, axis=0), jnp.min(x, axis=0)


def log_tile(x, rte, general):
    shape = x.shape
    x = folded(x)
    if general:
        value = psi_any(x) - jnp.log(rte)[None]
    else:
        w, g = psi_parts(x)
        value = (jnp.log(w) - jnp.log(rte)[None]) + g
    return value.reshape(shape).astype(BF16), jnp.min(x, axis=0)


def row_sum(x):
    return jnp.broadcast_to(jnp.sum(x, axis=0, keepdims=True), x.shape)


VMEM_SPEC = pl.BlockSpec(memory_space=pltpu.VMEM)
SMEM_SPEC = pl.BlockSpec(memory_space=pltpu.SMEM)
HBM_SPEC = pl.BlockSpec(memory_space=pltpu.HBM)
PARAMS = pltpu.CompilerParams(vmem_limit_bytes=24 * 2**20)


def in_hbm(x):
    return pltpu.with_memory_space_constraint(x, pltpu.HBM)


def in_vmem(x):
    return pltpu.with_memory_space_constraint(x, pltpu.VMEM)


def prepare_kernel(matchings_hbm, shape_hbm, item, *refs, last):
    choices, (matchings, shape, sems) = refs[:STRATA], refs[STRATA:]
    copies = [
        pltpu.make_async_copy(shape_hbm, shape, sems.at[0]),
        pltpu.make_async_copy(matchings_hbm, matchings, sems.at[1]),
    ]
    for copy in copies:
        copy.start()
    for copy in copies:
        copy.wait()
    item[...] = shape[...].astype(F32)
    choices[0][0] = matchings[0] - 1
    for stratum in range(1, STRATA - 1):
        choices[stratum][0] = jnp.bitwise_xor(matchings[stratum - 1], matchings[stratum]) - 1
    choices[STRATA - 1][0] = jnp.bitwise_xor(matchings[STRATA - 2], last) - 1


def prepare_call(matchings, item_shape, last):
    out = pl.pallas_call(
        functools.partial(prepare_kernel, last=last),
        out_shape=[jax.ShapeDtypeStruct(item_shape.shape, F32)]
        + [pltpu.SMEM((1,), jnp.int32)] * STRATA,
        in_specs=[HBM_SPEC, HBM_SPEC],
        out_specs=[VMEM_SPEC] + [SMEM_SPEC] * STRATA,
        scratch_shapes=[pltpu.SMEM(matchings.shape, jnp.int32), pltpu.VMEM(item_shape.shape, BF16),
                        pltpu.SemaphoreType.DMA((2,))],
        compiler_params=PARAMS,
        name="prepare",
    )(in_hbm(matchings), in_hbm(item_shape))
    return out[0], [choice[0] for choice in out[1:]]


def start_kernel(shape_hbm, interactions, theta, counts, *refs):
    uexps, (shape, sems) = refs[:-2], refs[-2:]
    depth = shape.shape[1]
    load = pltpu.make_async_copy(shape_hbm, shape, sems.at[0])
    ahead = pltpu.make_async_copy(interactions.at[0, pl.ds(0, counts.shape[0]), :], counts, sems.at[1])
    load.start()
    ahead.start()
    load.wait()
    total, low = jnp.zeros((8, depth), F32), jnp.ones((8, depth), F32)
    begin = 0
    for uexp in uexps:
        rows = uexp.shape[0]

        def step(i, carry, begin=begin, uexp=uexp):
            at = i * START_TILE
            x = shape[pl.ds(pl.multiple_of(begin + at, START_TILE), START_TILE), :].astype(F32)
            value, part, part_low = exp_tile(x, None, False)
            uexp[pl.ds(pl.multiple_of(at, START_TILE), START_TILE), :] = value
            return carry[0] + part, jnp.minimum(carry[1], part_low)

        total, low = lax.fori_loop(0, rows // START_TILE, step, (total, low))
        begin += rows
    theta[...] = total

    @pl.when(jnp.logical_not(above(low)))
    def _():
        begin = 0
        for uexp in uexps:

            def redo(at, size, _, begin=begin, uexp=uexp):
                x = shape[pl.ds(pl.multiple_of(begin + at, size), size), :].astype(F32)
                uexp[pl.ds(at, size), :] = exp_tile(x, None, True)[0]

            redo_loop(uexp.shape[0], redo)
            begin += uexp.shape[0]

    ahead.wait()


def start_call(user_shape, interactions, sizes):
    rows, depth = user_shape.shape
    items = interactions.shape[2]
    theta, counts, *uexps = pl.pallas_call(
        start_kernel,
        out_shape=[pltpu.VMEM((8, depth), F32), pltpu.VMEM((sizes[0], items), BF16)]
        + [pltpu.VMEM((size, depth), BF16) for size in sizes],
        in_specs=[HBM_SPEC] * 2,
        out_specs=[VMEM_SPEC] * (2 + len(sizes)),
        scratch_shapes=[pltpu.VMEM((rows, depth), BF16), pltpu.SemaphoreType.DMA((2,))],
        compiler_params=PARAMS,
        cost_estimate=pl.CostEstimate(
            flops=40 * rows * depth, bytes_accessed=rows * depth * 4, transcendentals=2 * rows * depth),
        name="user_start",
    )(in_hbm(user_shape), in_hbm(interactions))
    return theta, counts, uexps


def dot_rows(a, b):
    return lax.dot_general(a, b, (((1,), (1,)), ((), ())), preferred_element_type=F32)


def item_sums(ratios, uexp):
    return lax.dot_general(ratios[...], uexp[...], (((0,), (0,)), ((), ())), preferred_element_type=F32)


def stratum_kernel(names, *refs, stratum, at, rows, items, factor, first, last, earlier, cuts, ahead):
    ref = dict(zip(names, refs))
    copies = {}

    def fetch(name, source, target):
        copies[name] = pltpu.make_async_copy(source, target, ref["sems"].at[len(copies)])
        copies[name].start()

    if first and stratum > 0:
        fetch("item", ref["item"], ref["item_kept"])
    if ahead:
        fetch("ahead", ref["interactions"].at[ahead[0], pl.ds(ahead[1], ahead[2]), :], ref["counts_ahead"])
    upart, counts, ratios, denominator = ref["upart0"], ref["counts"], ref["ratios"], ref["denominator"]
    uexp = ref["uexp"]
    extra = 8 if first else 0

    lows = []
    theta = None
    item = ref["item_kept"] if first or last else None

    if stratum > 0:
        if first:
            beta = row_sum(ref["acc"][0:8, :] + ref["recv"][0:8, :])
            old = 1.0 if stratum == 1 else ref["rte_old"][...]
            rte = 0.5 * old + 0.5 * (0.3 + factor * beta)
            ref["rte_new"][...] = rte
        else:
            rte = ref["rte"][...]
        lows.append(usual(rte))
        for t, step in tiles(rows):
            old = ref["user_shape"][at + t:at + t + step, :].astype(F32) if stratum == 1 else ref["shp_old"][t:t + step, :]
            stat = ref["acc"][extra + t:extra + t + step, :] + ref["recv"][extra + t:extra + t + step, :]
            shp = 0.5 * old + 0.5 * (0.3 + factor * stat)
            ref["shp_new"][t:t + step, :] = shp
            value, part, low = exp_tile(shp, rte, False)
            uexp[t:t + step, :] = value
            theta = part if theta is None else theta + part
            lows.append(low)
        if not first:
            theta = theta + ref["theta"][...]
        total_mean = ref["theta_new"]
        total_mean[...] = theta
    elif last:
        total_mean = ref["theta"]

    if first and stratum > 0:
        copies["item"].wait()
    elif first:
        item[...] = ref["item"][...]
        uexp[...] = ref["uexp_in"][...]
    if first or last:
        item_rte = None if stratum == 0 else item[items:items + 8, :]
    if first:
        item_exp, sums, low = exp_tile(item[0:items, :], item_rte, False)
        ref["item_exp_new"][...] = item_exp
        upart[0:8, :] = sums
        lows.append(low)
        if item_rte is not None:
            lows.append(usual(item_rte))
    else:
        item_exp = ref["item_exp"][...]

    denominator[...] = dot_rows(uexp[...], item_exp)
    for t, step in tiles(rows):
        ratios[t:t + step, :] = (
            counts[t:t + step, :].astype(F32) / denominator[t:t + step, :]).astype(BF16)
    user_sums = uexp[...].astype(F32) * jnp.dot(ratios[...], item_exp, preferred_element_type=F32)
    parts = []
    for i, length in enumerate(cuts):
        begin, skip = sum(cuts[:i]), 0 if i else extra
        parts.append((ref[f"upart{i}"], begin, skip, length))
        parts[i][0][skip:skip + length, :] = user_sums[begin:begin + length, :]
    pairs = [(ref[f"ratios{i}"], ref[f"uexp{i}"]) for i in range(earlier)] + [(ratios, uexp)]

    def update_items(istat):
        old = 1.0 if item_rte is None else item_rte
        kept = ref["item_exp_new" if first else "item_exp"][...].astype(F32)
        ref["item_new"][0:items, :] = 0.5 * item[0:items, :] + 0.5 * (0.3 + factor * (kept * istat))
        ref["item_new"][items:items + 8, :] = 0.5 * old + 0.5 * (0.3 + factor * row_sum(total_mean[...]))

    if last:
        istat = None
        for pair in pairs:
            part = item_sums(*pair)
            istat = part if istat is None else istat + part
        update_items(istat)

    if lows:

        @pl.when(jnp.logical_not(above(functools.reduce(jnp.minimum, lows))))
        def _():
            if stratum > 0:

                def redo_users(at, size, total):
                    place = pl.ds(at, size)
                    uexp[place, :], part, _ = exp_tile(ref["shp_new"][place, :], rte, True)
                    return total + part

                start = jnp.zeros_like(rte) if first else ref["theta"][...]
                total_mean[...] = redo_loop(rows, redo_users, start)
            if first:

                def redo_items(at, size, total):
                    place = pl.ds(at, size)
                    ref["item_exp_new"][place, :], part, _ = exp_tile(item[place, :], item_rte, True)
                    return total + part

                upart[0:8, :] = redo_loop(items, redo_items, jnp.zeros((8, upart.shape[1]), F32))
            kept = ref["item_exp_new" if first else "item_exp"]
            for target, begin, skip, length in parts:

                def redo_sums(at, size, _, target=target, begin=begin, skip=skip):
                    place = pl.ds(pl.multiple_of(begin + at, size), size)
                    u = uexp[place, :]
                    ratio = (counts[place, :].astype(F32) / dot_rows(u, kept[...])).astype(BF16)
                    ratios[place, :] = ratio
                    target[pl.ds(pl.multiple_of(skip + at, 8), size), :] = u.astype(F32) * jnp.dot(
                        ratio, kept[...], preferred_element_type=F32)

                redo_loop(length, redo_sums)
            if last:
                total = ref["item_new"].at[pl.ds(0, items), :]
                total[...] = jnp.zeros((items, ref["item_new"].shape[1]), F32)
                for pair in pairs:

                    def redo_stat(at, size, _, pair=pair):
                        place = pl.ds(at, size)
                        total[...] += item_sums(pair[0].at[place, :], pair[1].at[place, :])

                    redo_loop(rows if pair[0] is ratios else pair[0].shape[0], redo_stat)
                update_items(total[...])

    if ahead:
        copies["ahead"].wait()


def stratum_call(stratum, at, rows, items, depth, factor, first, last, earlier, cuts, ahead, operands):
    extra = 8 if first else 0
    outs = {f"upart{i}": ((size + (0 if i else extra), depth), F32) for i, size in enumerate(cuts)}
    if stratum > 0:
        outs["shp_new"] = ((rows, depth), F32)
    if first and stratum > 0:
        outs["rte_new"] = ((8, depth), F32)
    if first:
        outs["item_exp_new"] = ((items, depth), BF16)
    if first:
        outs["item_kept"] = (operands["item"].shape, F32)
    if last:
        outs["item_new"] = ((items + 8, depth), F32)
    else:
        outs["ratios"] = ((rows, items), BF16)
        outs["uexp"] = ((rows, depth), BF16)
        if stratum > 0:
            outs["theta_new"] = ((8, depth), F32)
    if ahead:
        outs["counts_ahead"] = ((ahead[2], items), BF16)
    scratch = {
        "denominator": pltpu.VMEM((rows, items), F32),
        "sems": pltpu.SemaphoreType.DMA((2,)),
    }
    if last:
        scratch["ratios"] = pltpu.VMEM((rows, items), BF16)
        if stratum > 0:
            scratch["uexp"] = pltpu.VMEM((rows, depth), BF16)
            scratch["theta_new"] = pltpu.VMEM((8, depth), F32)
    hbm = ("interactions", "item") if stratum > 0 else ("interactions",)
    operands = {
        name: in_hbm(x) if name in hbm else in_vmem(x) if name in ("user_shape", "item") else x
        for name, x in operands.items()}
    names = list(operands) + list(outs) + list(scratch)
    kernel = functools.partial(
        stratum_kernel, names, stratum=stratum, at=at, rows=rows, items=items,
        factor=factor, first=first, last=last, earlier=earlier, cuts=cuts, ahead=ahead)
    results = pl.pallas_call(
        kernel,
        out_shape=[jax.ShapeDtypeStruct(*spec) for spec in outs.values()],
        in_specs=[HBM_SPEC if name in hbm else VMEM_SPEC for name in operands],
        out_specs=[VMEM_SPEC] * len(outs),
        scratch_shapes=list(scratch.values()),
        compiler_params=PARAMS,
        cost_estimate=pl.CostEstimate(
            flops=600 * rows * items * depth, bytes_accessed=rows * 200000, transcendentals=rows * depth),
        name=f"stratum{stratum}_at{at}",
    )(*operands.values())
    return dict(zip(outs, results))


def user_log_kernel(*refs, at, rows, shp_at, factor, first, filled):
    acc, recv, shp_old, rte_in = refs[:4]
    rest = refs[5:] if filled else refs[4:]
    out, *rte_out, block, sem = rest
    rte = rte_in[...]
    if first:
        rte = 0.5 * rte + 0.5 * (0.3 + factor * row_sum(acc[0:8, :] + recv[0:8, :]))
    for ref in rte_out:
        ref[...] = rte
    extra = 8 if first else 0

    def shape(t, step):
        stat = acc[pl.ds(extra + t, step), :] + recv[pl.ds(extra + t, step), :]
        return 0.5 * shp_old[pl.ds(shp_at + t, step), :] + 0.5 * (0.3 + factor * stat)

    low = rte
    for t, step in tiles(rows):
        block[t:t + step, :], part_low = log_tile(shape(t, step), rte, False)
        low = jnp.minimum(low, part_low)

    @pl.when(jnp.logical_not(above(low)))
    def _():
        def redo(t, step, _):
            block[pl.ds(t, step), :] = log_tile(shape(pl.multiple_of(t, 8), step), rte, True)[0]

        redo_loop(rows, redo)

    copy = pltpu.make_async_copy(block, out.at[pl.ds(at, rows), :], sem)
    copy.start()
    copy.wait()


def user_log_call(at, rows, shp_at, total, depth, factor, first, operands, filled):
    out_shape = [jax.ShapeDtypeStruct((total, depth), BF16)]
    out_specs = [HBM_SPEC]
    if at + rows < total:
        out_shape.append(jax.ShapeDtypeStruct((8, depth), F32))
        out_specs.append(VMEM_SPEC)
    operands = list(operands)
    in_specs = [VMEM_SPEC] * 4
    if filled is not None:
        operands.append(filled)
        in_specs.append(HBM_SPEC)
    return pl.pallas_call(
        functools.partial(user_log_kernel, at=at, rows=rows, shp_at=shp_at, factor=factor, first=first,
                          filled=filled is not None),
        out_shape=out_shape,
        in_specs=in_specs,
        out_specs=out_specs,
        input_output_aliases={} if filled is None else {4: 0},
        scratch_shapes=[pltpu.VMEM((rows, depth), BF16), pltpu.SemaphoreType.DMA],
        compiler_params=PARAMS,
        cost_estimate=pl.CostEstimate(
            flops=40 * rows * depth, bytes_accessed=rows * depth * 14, transcendentals=rows * depth),
        name=f"user_log_at{at}",
    )(*operands)


def item_log_kernel(item, through, out, passed, *, items):
    passed[...] = through[...]
    rte = item[items:items + 8, :]

    out[...], low = log_tile(item[0:items, :], rte, False)

    @pl.when(jnp.logical_not(above(jnp.minimum(low, rte))))
    def _():
        def redo(t, step, _):
            place = pl.ds(t, step)
            out[place, :] = log_tile(item[place, :], rte, True)[0]

        redo_loop(items, redo)


def item_log_call(item, through, items, depth):
    return pl.pallas_call(
        functools.partial(item_log_kernel, items=items),
        out_shape=[jax.ShapeDtypeStruct((items, depth), BF16), jax.ShapeDtypeStruct(through.shape, F32)],
        in_specs=[VMEM_SPEC, VMEM_SPEC],
        out_specs=[VMEM_SPEC, VMEM_SPEC],
        compiler_params=PARAMS,
        cost_estimate=pl.CostEstimate(
            flops=40 * items * depth, bytes_accessed=items * depth * 6, transcendentals=items * depth),
        name="item_log",
    )(item, through)


def swapped(value, axis, mask):
    return lax.ppermute(value, axis, [(a, a ^ mask) for a in range(lax.axis_size(axis))])


def moved(choice, value, then=None, operands=()):
    def branch(mask, value, *operands):
        arrived = swapped(value, "users", mask)
        return arrived if then is None else then(arrived, *operands)

    choices = [functools.partial(branch, mask) for mask in range(1, lax.axis_size("users"))]
    return lax.switch(choice, choices, value, *operands)


def exchanged(value):
    size = lax.axis_size("items")
    if size == 1:
        return value, jnp.zeros_like(value)
    mask = 1
    while mask * 2 < size:
        value = value + swapped(value, "items", mask)
        mask *= 2
    return value, swapped(value, "items", mask)


def per_device(interactions, matchings, user_shape, item_shape):
    group = lax.axis_size("users")
    factor = float(group)
    users, depth = user_shape.shape
    items = item_shape.shape[0]
    sizes = chunk_rows(users)
    starts = [sum(sizes[:i]) for i in range(len(sizes))]
    count = len(sizes)

    item, choices = prepare_call(matchings, item_shape, group - 1)
    order = [(s, at, rows) for s in range(STRATA) for at, rows in zip(starts, sizes)]

    def opening(arrived, user_shape, interactions):
        theta, counts, uexps = start_call(user_shape, interactions, sizes)
        operands = {"counts": counts, "interactions": interactions, "uexp_in": uexps[0], "item": arrived}
        if count == 1:
            operands["theta"] = theta
        out = stratum_call(
            0, 0, sizes[0], items, depth, factor, True, count == 1, 0, sizes[:1], order[1], operands)
        return theta, [out["uexp"], *uexps[1:]], out

    theta, uexps, opened = moved(choices[0], item, opening, (user_shape, interactions))
    rte = None
    shp = [None] * count
    sums = [None] * count
    for stratum in range(STRATA):
        carried = {"theta": theta}
        earlier = {}
        for i, (at, rows) in enumerate(zip(starts, sizes)):
            first, last = i == 0, i == count - 1
            step = stratum * count + i
            ahead = order[step + 1] if step + 1 < len(order) else None
            cuts = last_cuts(rows) if step + 1 == len(order) else [rows]
            operands = {"counts": counts} if step else {}
            if ahead:
                operands["interactions"] = interactions
            if stratum == 0:
                operands["uexp"] = uexps[i]
            else:
                operands["acc"], operands["recv"] = sums[i]
                if stratum == 1:
                    operands["user_shape"] = user_shape
                else:
                    operands["shp_old"] = shp[i]
                if not first:
                    operands["rte"] = rte
                elif stratum > 1:
                    operands["rte_old"] = rte
            if first:
                operands["item"] = item
            elif last:
                operands["item_kept"] = carried["item_kept"]
            if not first:
                operands["item_exp"] = carried["item_exp"]
            if last:
                operands.update(earlier)
            if (stratum > 0 and not first) or (stratum == 0 and last):
                operands["theta"] = carried["theta"]
            if step == 0:
                out = opened
            else:
                out = stratum_call(
                    stratum, at, rows, items, depth, factor, first, last, i, cuts, ahead, operands)
            counts = out.get("counts_ahead")
            shp[i] = out.get("shp_new")
            sums[i] = exchanged(out["upart0"])
            if first:
                rte = out.get("rte_new")
                carried["item_exp"] = out["item_exp_new"]
                carried["item_kept"] = out["item_kept"]
            if last:
                item = out["item_new"]
            else:
                earlier[f"ratios{i}"], earlier[f"uexp{i}"] = out["ratios"], out.get("uexp", operands.get("uexp"))
                if stratum > 0:
                    carried["theta"] = out["theta_new"]
        if stratum + 1 < STRATA:
            item = moved(choices[stratum + 1], item)
        else:
            item = swapped(item, "users", group - 1)
    user_log = None
    pieces = [(at, rows, 0, sums[i], shp[i]) for i, (at, rows) in enumerate(zip(starts, sizes))]
    pieces[-1:] = [
        (starts[-1] + sum(cuts[:i]), size, sum(cuts[:i]), exchanged(out[f"upart{i}"]) if i else sums[-1], shp[-1])
        for i, size in enumerate(cuts)]
    for i, (at, rows, shp_at, piece_sums, piece_shp) in enumerate(pieces):
        user_log, *rest = user_log_call(
            at, rows, shp_at, users, depth, factor, i == 0, (*piece_sums, piece_shp, rte), user_log)
        rte = rest[0] if rest else rte
        if i == max(len(pieces) - 3, 0):
            item_log, rte = item_log_call(item, rte, items, depth)
    return user_log, item_log


def solution(mesh):
    placed = (P(None, "users", "items"), P(), P("users", None), P(("users", "items"), None))
    return jax.shard_map(
        per_device,
        mesh=mesh,
        in_specs=placed,
        out_specs=(P("users", None), P(("users", "items"), None)),
        check_vma=False,
    )
```

profile of v0, /device:TPU:1, one launch (start us, length us, event | category | flops | bytes accessed | tf_op | source)
XLA Modules:
  0.0 58.6 jit_solution(3917221823902580593)
XLA Ops:
  0.6 0.9 %prepare.1 = (f32[256,128]{1,0:T(8,128)S(1)}, s32[1]{0:T(128)S(4)}, s32[1]{0:T(128)S(4)}, s32[1]{0:T(128)S(4)}) custom-call(s32[3]{0:T(128)} %matchings_hbm.1, bf16[256,128]{1,0:T(8,128)(2,1)} %shape_hbm.1), custom_call_target="tpu_custom_call" | custom-call | tf_op jit(solution)/shard_map/prepare/pallas_call | solution.py:151
  1.5 6.6 %conditional.3 = (f32[8,128]{1,0:T(8,128)S(1)}, bf16[896,128]{1,0:T(8,128)(2,1)S(1)}, bf16[896,256]{1,0:T(8,128)(2,1)S(1)}, bf16[256,128]{1,0:T(8,128)(2,1)S(1)}...) conditional(s32[]{:T(128)} %bitcast, ...), branch_computations={%region_0.0_spmd, %region_1.0_spmd, %region_2.0_spmd, %region_3.0_... | conditional | flops 7556300800 | bytes 77979752 | solution.py:513
  1.6 2.1 %collective-permute-start.1 = (f32[256,128]{1,0:T(8,128)S(1)}, f32[256,128]{1,0:T(8,128)S(1)}, u32[]{:S(2)}, u32[]{:S(2)}) collective-permute-start(f32[256,128]{1,0:T(8,128)S(1)} %get-tuple-element.171), channel_id=1, source_target_pairs={{0,4},{2,6},{4,0},{6,2},{8,12},{10,14},{12,8},{14,10},{16,20},{18,... | collective-permute-start | bytes 393224 | tf_op jit(solution)/shard_map/cond/branch_1_fun/ppermute | solution.py:504
  3.7 2.0 %user_start.16 = (f32[8,128]{1,0:T(8,128)S(1)}, bf16[384,256]{1,0:T(8,128)(2,1)S(1)}, bf16[384,128]{1,0:T(8,128)(2,1)S(1)}, bf16[896,128]{1,0:T(8,128)(2,1)S(1)}) custom-call(bf16[1280,128]{1,0:T(8,128)(2,1)} %get-tuple-element.165.shape_hbm, bf16[3,1280,256]{2,1,0:T(8,128)(2,1)} %get-tuple-element.166.interactions.refs_1_), custom_call_target="tpu_custom_call" | custom-call | flops 6553600 | bytes 655360 | tf_op jit(solution)/shard_map/cond/branch_1_fun/user_start/pallas_call | solution.py:207
  5.7 1.3 %collective-permute-done.1.refs_3_ = f32[256,128]{1,0:T(8,128)S(1)} collective-permute-done((f32[256,128]{1,0:T(8,128)S(1)}, f32[256,128]{1,0:T(8,128)S(1)}, u32[]{:S(2)}, u32[]{:S(2)}) %collective-permute-start.1) | collective-permute-done | bytes 131104 | tf_op jit(solution)/shard_map/cond/branch_1_fun/ppermute | solution.py:504
  6.9 1.0 %stratum0_at0.16 = (f32[392,128]{1,0:T(8,128)S(1)}, bf16[256,128]{1,0:T(8,128)(2,1)S(1)}, f32[256,128]{1,0:T(8,128)S(1)}, bf16[384,256]{1,0:T(8,128)(2,1)S(1)}, ...) custom-call(bf16[384,256]{1,0:T(8,128)(2,1)S(1)} %get-tuple-element.169.refs_0_, ...), custom_call_target="tpu_custom_call" | custom-call | flops 7549747200 | bytes 76800000 | tf_op jit(solution)/shard_map/cond/branch_1_fun/stratum0_at0/pallas_call | solution.py:403
  8.2 1.2 %collective-permute-start.45 = (f32[392,128]{1,0:T(8,128)S(1)}, f32[392,128]{1,0:T(8,128)S(1)}, u32[]{:S(2)}, u32[]{:S(2)}) collective-permute-start(f32[392,128]{1,0:T(8,128)S(1)} %get-tuple-element.412.refs_2_), channel_id=1, source_target_pairs={{0,1},{1,0},{2,3},{3,2},{4,5},{5,4},{6,7},{7,6},{8,9},{9,8},{10,11... | collective-permute-start | bytes 602120 | tf_op jit(solution)/shard_map/ppermute | solution.py:504
  9.3 0.0 copy-start
  9.3 1.0 %stratum0_at384.1 = (f32[896,128]{1,0:T(8,128)S(1)}, f32[264,128]{1,0:T(8,128)S(1)}, bf16[384,256]{1,0:T(8,128)(2,1)S(1)}) custom-call(bf16[896,256]{1,0:T(8,128)(2,1)S(1)} %get-tuple-element.404.refs_0_, bf16[3,1280,256]{2,1,0:T(8,128)(2,1)} %refs_1_.7, bf16[896,128]{1,0:T(8,128)(2,1)S(1)} %get-tuple-element.405.refs_2_, ...), custom_call_target="tpu_custom_call" | custom-call | flops 17616076800 | bytes 179200000 | tf_op jit(solution)/shard_map/stratum0_at384/pallas_call | solution.py:403
  10.3 0.4 collective-permute-start.46
  10.8 4.2 %conditional.4 = (f32[264,128]{1,0:T(8,128)}) conditional(s32[]{:T(128)} %bitcast.1, f32[264,128]{1,0:T(8,128)S(1)} %get-tuple-element.414, f32[264,128]{1,0:T(8,128)S(1)} %get-tuple-element.414, f32[264,128]{1,0:T(8,128)S(1)} %get-tuple-element.414, f32[264,128]{1,0:T(8,128)S(1)} %get-tuple-element.414, ...), branch_computations={%region_15.0_spmd, %region_16.0_spmd, %region_17.0_spmd, %region_1... | conditional | bytes 540720 | solution.py:513
  10.8 1.2 %collective-permute-start.18 = (f32[264,128]{1,0:T(8,128)S(1)}, f32[264,128]{1,0:T(8,128)}, u32[]{:S(2)}, u32[]{:S(2)}) collective-permute-start(f32[264,128]{1,0:T(8,128)S(1)} %param.18), channel_id=1, source_target_pairs={{0,8},{2,10},{4,12},{6,14},{8,0},{10,2},{12,4},{14,6},{16,24},{18,... | collective-permute-start | bytes 405512 | tf_op jit(solution)/shard_map/cond/branch_3_fun/ppermute | solution.py:504
  12.0 3.0 %collective-permute-done.18 = f32[264,128]{1,0:T(8,128)} collective-permute-done((f32[264,128]{1,0:T(8,128)S(1)}, f32[264,128]{1,0:T(8,128)}, u32[]{:S(2)}, u32[]{:S(2)}) %collective-permute-start.18) | collective-permute-done | bytes 135200 | tf_op jit(solution)/shard_map/cond/branch_3_fun/ppermute | solution.py:504
  14.9 0.0 collective-permute-done.45.refs_3_
  14.9 0.0 copy-done
  14.9 1.4 %stratum1_at0.1 = (f32[392,128]{1,0:T(8,128)S(1)}, f32[384,128]{1,0:T(8,128)S(1)}, f32[8,128]{1,0:T(8,128)S(1)}, bf16[256,128]{1,0:T(8,128)(2,1)S(1)}, f32[264,1...) custom-call(bf16[384,256]{1,0:T(8,128)(2,1)S(1)} %get-tuple-element., ...), custom_call_target="tpu_custom_call" | custom-call | flops 7549747200 | bytes 76800000 | tf_op jit(solution)/shard_map/stratum1_at0/pallas_call | solution.py:403
  16.4 1.2 %collective-permute-start.47 = (f32[392,128]{1,0:T(8,128)S(1)}, f32[392,128]{1,0:T(8,128)S(1)}, u32[]{:S(2)}, u32[]{:S(2)}) collective-permute-start(f32[392,128]{1,0:T(8,128)S(1)} %get-tuple-element.424.refs_2_), channel_id=1, source_target_pairs={{0,1},{1,0},{2,3},{3,2},{4,5},{5,4},{6,7},{7,6},{8,9},{9,8},{10,11... | collective-permute-start | bytes 602120 | tf_op jit(solution)/shard_map/ppermute | solution.py:504
  17.6 5.8 %collective-permute-done.46.refs_3_ = f32[896,128]{1,0:T(8,128)S(1)} collective-permute-done((f32[896,128]{1,0:T(8,128)S(1)}, f32[896,128]{1,0:T(8,128)S(1)}, u32[]{:S(2)}, u32[]{:S(2)}) %collective-permute-start.46) | collective-permute-done | bytes 458784 | tf_op jit(solution)/shard_map/ppermute | solution.py:504
  23.3 1.3 %stratum1_at384.1 = (f32[896,128]{1,0:T(8,128)S(1)}, f32[896,128]{1,0:T(8,128)S(1)}, f32[264,128]{1,0:T(8,128)S(1)}, bf16[384,256]{1,0:T(8,128)(2,1)S(1)}) custom-call(bf16[896,256]{1,0:T(8,128)(2,1)S(1)} %get-tuple-element.415.refs_0_, bf16[3,1280,256]{2,1,0:T(8,128)(2,1)} %refs_1_.7, f32[896,128]{1,0:T(8,128)S(1)} %get-tuple-element.416.refs_2_, ...), custom_call_target="tpu_custom_call" | custom-call | flops 17616076800 | bytes 179200000 | tf_op jit(solution)/shard_map/stratum1_at384/pallas_call | solution.py:403
  24.6 0.8 %collective-permute-start.48 = (f32[896,128]{1,0:T(8,128)S(1)}, f32[896,128]{1,0:T(8,128)S(1)}, u32[]{:S(2)}, u32[]{:S(2)}) collective-permute-start(f32[896,128]{1,0:T(8,128)S(1)} %get-tuple-element.429.refs_1_), channel_id=1, source_target_pairs={{0,1},{1,0},{2,3},{3,2},{4,5},{5,4},{6,7},{7,6},{8,9},{9,8},{10,11... | collective-permute-start | bytes 1376264 | tf_op jit(solution)/shard_map/ppermute | solution.py:504
  25.5 14.0 %conditional.5 = (f32[264,128]{1,0:T(8,128)}) conditional(s32[]{:T(128)} %bitcast.2, f32[264,128]{1,0:T(8,128)S(1)} %get-tuple-element.427, f32[264,128]{1,0:T(8,128)S(1)} %get-tuple-element.427, f32[264,128]{1,0:T(8,128)S(1)} %get-tuple-element.427, f32[264,128]{1,0:T(8,128)S(1)} %get-tuple-element.427, ...), branch_computations={%region_30.0_spmd, %region_31.0_spmd, %region_32.0_spmd, %region_3... | conditional | bytes 540720 | solution.py:513
  25.5 7.0 %collective-permute-start.38 = (f32[264,128]{1,0:T(8,128)S(1)}, f32[264,128]{1,0:T(8,128)}, u32[]{:S(2)}, u32[]{:S(2)}) collective-permute-start(f32[264,128]{1,0:T(8,128)S(1)} %param.38), channel_id=1, source_target_pairs={{0,18},{2,16},{4,22},{6,20},{8,26},{10,24},{12,30},{14,28},{16,2},... | collective-permute-start | bytes 405512 | tf_op jit(solution)/shard_map/cond/branch_8_fun/ppermute | solution.py:504
  32.5 7.0 %collective-permute-done.38 = f32[264,128]{1,0:T(8,128)} collective-permute-done((f32[264,128]{1,0:T(8,128)S(1)}, f32[264,128]{1,0:T(8,128)}, u32[]{:S(2)}, u32[]{:S(2)}) %collective-permute-start.38) | collective-permute-done | bytes 135200 | tf_op jit(solution)/shard_map/cond/branch_8_fun/ppermute | solution.py:504
  39.5 0.0 collective-permute-done.47.refs_3_
  39.5 1.4 %stratum2_at0.1 = (f32[392,128]{1,0:T(8,128)S(1)}, f32[384,128]{1,0:T(8,128)S(1)}, f32[8,128]{1,0:T(8,128)S(1)}, bf16[256,128]{1,0:T(8,128)(2,1)S(1)}, f32[264,1...) custom-call(bf16[384,256]{1,0:T(8,128)(2,1)S(1)} %get-tuple-element., ...), custom_call_target="tpu_custom_call" | custom-call | flops 7549747200 | bytes 76800000 | tf_op jit(solution)/shard_map/stratum2_at0/pallas_call | solution.py:403
  40.9 0.1 collective-permute-start.54
  41.0 0.0 collective-permute-done.48.refs_2_
  41.0 1.3 %stratum2_at384.1 = (f32[256,128]{1,0:T(8,128)S(1)}, f32[256,128]{1,0:T(8,128)S(1)}, f32[192,128]{1,0:T(8,128)S(1)}, f32[192,128]{1,0:T(8,128)S(1)}, f32[896,128]{1,0:T(8,128)S(1)}, /*index=5*/f32[264,128]{1,0:T(8,128)S(1)}) custom-call(bf16[896,256]{1,0:T(8,128)(2,1)S(1)} %get-tuple-element.428.refs_0_, f32[896,128]{1,0:T(8,128)S(1)} %get-tuple-element.429.refs_1_, ...), custom_call_target="tpu_custom_call" | custom-call | flops 17616076800 | bytes 179200000 | tf_op jit(solution)/shard_map/stratum2_at384/pallas_call | solution.py:403
  42.3 3.2 %collective-permute-start.51 = (f32[264,128]{1,0:T(8,128)S(1)}, f32[264,128]{1,0:T(8,128)S(1)}, u32[]{:S(2)}, u32[]{:S(2)}) collective-permute-start(f32[264,128]{1,0:T(8,128)S(1)} %get-tuple-element.440), channel_id=1, source_target_pairs={{0,30},{2,28},{4,26},{6,24},{8,22},{10,20},{12,18},{14,16},{16,14}... | collective-permute-start | bytes 405512 | tf_op jit(solution)/shard_map/ppermute | solution.py:504
  45.5 1.3 %collective-permute-start.53 = (f32[256,128]{1,0:T(8,128)S(1)}, f32[256,128]{1,0:T(8,128)S(1)}, u32[]{:S(2)}, u32[]{:S(2)}) collective-permute-start(f32[256,128]{1,0:T(8,128)S(1)} %get-tuple-element.442.refs_0_), channel_id=1, source_target_pairs={{0,1},{1,0},{2,3},{3,2},{4,5},{5,4},{6,7},{7,6},{8,9},{9,8},{10,11... | collective-permute-start | bytes 393224 | tf_op jit(solution)/shard_map/ppermute | solution.py:504
  46.7 0.2 collective-permute-start.52
  46.9 1.3 %collective-permute-start.50 = (f32[192,128]{1,0:T(8,128)S(1)}, f32[192,128]{1,0:T(8,128)S(1)}, u32[]{:S(2)}, u32[]{:S(2)}) collective-permute-start(f32[192,128]{1,0:T(8,128)S(1)} %get-tuple-element.439.refs_0_), channel_id=1, source_target_pairs={{0,1},{1,0},{2,3},{3,2},{4,5},{5,4},{6,7},{7,6},{8,9},{9,8},{10,11... | collective-permute-start | bytes 294920 | tf_op jit(solution)/shard_map/ppermute | solution.py:504
  48.2 0.0 collective-permute-done.54.refs_1_
  48.2 0.2 collective-permute-start.49
  48.4 1.0 %user_log_at0.1 = (bf16[1280,128]{1,0:T(8,128)(2,1)}, f32[8,128]{1,0:T(8,128)S(1)}) custom-call(f32[392,128]{1,0:T(8,128)S(1)} %get-tuple-element.443.refs_0_, f32[392,128]{1,0:T(8,128)S(1)} %collective-permute-done.54.refs_1_, f32[384,128]{1,0:T(8,128)S(1)} %get-tuple-element.444.refs_2_, f32[8,128]{1,0:T(8,128)S(1)} %get-tuple-element.431.refs_4_.refs_3_), custom_call_target="tpu_custom_call" | custom-call | flops 1966080 | bytes 688128 | tf_op jit(solution)/shard_map/user_log_at0/pallas_call | solution.py:460
  49.5 1.6 %collective-permute-done.53.refs_1_ = f32[256,128]{1,0:T(8,128)S(1)} collective-permute-done((f32[256,128]{1,0:T(8,128)S(1)}, f32[256,128]{1,0:T(8,128)S(1)}, u32[]{:S(2)}, u32[]{:S(2)}) %collective-permute-start.53) | collective-permute-done | bytes 131104 | tf_op jit(solution)/shard_map/ppermute | solution.py:504
  51.1 0.9 %user_log_at384.1 = (bf16[1280,128]{1,0:T(8,128)(2,1)}, f32[8,128]{1,0:T(8,128)S(1)}) custom-call(f32[256,128]{1,0:T(8,128)S(1)} %get-tuple-element.442.refs_0_, f32[256,128]{1,0:T(8,128)S(1)} %collective-permute-done.53.refs_1_, f32[896,128]{1,0:T(8,128)S(1)} %get-tuple-element.438.refs_2_, ...), custom_call_target="tpu_custom_call", output_to_operand_aliasing={{0}: (4, {})} | custom-call | flops 1310720 | bytes 458752 | tf_op jit(solution)/shard_map/user_log_at384/pallas_call | solution.py:460
  52.0 1.9 %collective-permute-done.52.refs_1_ = f32[256,128]{1,0:T(8,128)S(1)} collective-permute-done((f32[256,128]{1,0:T(8,128)S(1)}, f32[256,128]{1,0:T(8,128)S(1)}, u32[]{:S(2)}, u32[]{:S(2)}) %collective-permute-start.52) | collective-permute-done | bytes 131104 | tf_op jit(solution)/shard_map/ppermute | solution.py:504
  53.9 0.9 %user_log_at640.1 = (bf16[1280,128]{1,0:T(8,128)(2,1)}, f32[8,128]{1,0:T(8,128)S(1)}) custom-call(f32[256,128]{1,0:T(8,128)S(1)} %get-tuple-element.441.refs_0_, f32[256,128]{1,0:T(8,128)S(1)} %collective-permute-done.52.refs_1_, f32[896,128]{1,0:T(8,128)S(1)} %get-tuple-element.438.refs_2_, ...), custom_call_target="tpu_custom_call", output_to_operand_aliasing={{0}: (4, {})} | custom-call | flops 1310720 | bytes 458752 | tf_op jit(solution)/shard_map/user_log_at640/pallas_call | solution.py:460
  54.8 0.0 collective-permute-done.51.item
  54.8 0.9 %item_log.1 = (bf16[256,128]{1,0:T(8,128)(2,1)}, f32[8,128]{1,0:T(8,128)S(1)}) custom-call(f32[264,128]{1,0:T(8,128)S(1)} %collective-permute-done.51.item, f32[8,128]{1,0:T(8,128)S(1)} %get-tuple-element.449.through), custom_call_target="tpu_custom_call" | custom-call | flops 1310720 | bytes 196608 | tf_op jit(solution)/shard_map/item_log/pallas_call | solution.py:491
  55.8 0.2 collective-permute-done.50.refs_1_
  56.0 0.9 %user_log_at896.1 = (bf16[1280,128]{1,0:T(8,128)(2,1)}, f32[8,128]{1,0:T(8,128)S(1)}) custom-call(f32[192,128]{1,0:T(8,128)S(1)} %get-tuple-element.439.refs_0_, f32[192,128]{1,0:T(8,128)S(1)} %collective-permute-done.50.refs_1_, f32[896,128]{1,0:T(8,128)S(1)} %get-tuple-element.438.refs_2_, ...), custom_call_target="tpu_custom_call", output_to_operand_aliasing={{0}: (4, {})} | custom-call | flops 983040 | bytes 344064 | tf_op jit(solution)/shard_map/user_log_at896/pallas_call | solution.py:460
  56.9 0.7 %collective-permute-done.49.refs_1_ = f32[192,128]{1,0:T(8,128)S(1)} collective-permute-done((f32[192,128]{1,0:T(8,128)S(1)}, f32[192,128]{1,0:T(8,128)S(1)}, u32[]{:S(2)}, u32[]{:S(2)}) %collective-permute-start.49) | collective-permute-done | bytes 98336 | tf_op jit(solution)/shard_map/ppermute | solution.py:504
  57.6 0.9 %user_log_at1088.1 = bf16[1280,128]{1,0:T(8,128)(2,1)} custom-call(f32[192,128]{1,0:T(8,128)S(1)} %get-tuple-element.437.refs_0_, f32[192,128]{1,0:T(8,128)S(1)} %collective-permute-done.49.refs_1_, f32[896,128]{1,0:T(8,128)S(1)} %get-tuple-element.438.refs_2_, f32[8,128]{1,0:T(8,128)S(1)} %get-tuple-element.452.refs_3_, ...), custom_call_target="tpu_custom_call", output_to_operand_aliasing={{}: (4, {})} | custom-call | flops 983040 | bytes 344064 | tf_op jit(solution)/shard_map/user_log_at1088/pallas_call | solution.py:460
Async XLA Ops:
  1.6 5.4 %collective-permute-start.1 = (f32[256,128]{1,0:T(8,128)S(1)}, f32[256,128]{1,0:T(8,128)S(1)}, u32[]{:S(2)}, u32[]{:S(2)}) collective-permute-start(f32[256,128]{1,0:T(8,128)S(1)} %get-tuple-element.171), channel_id=1, source_target_pairs={{0,4},{2,6},{4,0},{6,2},{8,12},{10,14},{12,8},{14,10},{16,20},{18,... | collective-permute-start | bytes 393224 | tf_op jit(solution)/shard_map/cond/branch_1_fun/ppermute | solution.py:504
  8.2 6.8 %collective-permute-start.45 = (f32[392,128]{1,0:T(8,128)S(1)}, f32[392,128]{1,0:T(8,128)S(1)}, u32[]{:S(2)}, u32[]{:S(2)}) collective-permute-start(f32[392,128]{1,0:T(8,128)S(1)} %get-tuple-element.412.refs_2_), channel_id=1, source_target_pairs={{0,1},{1,0},{2,3},{3,2},{4,5},{5,4},{6,7},{7,6},{8,9},{9,8},{10,11... | collective-permute-start | bytes 602120 | tf_op jit(solution)/shard_map/ppermute | solution.py:504
  9.3 5.6 %copy-start = (bf16[1280,128]{1,0:T(8,128)(2,1)S(1)}, bf16[1280,128]{1,0:T(8,128)(2,1)}, u32[]{:S(2)}) copy-start(bf16[1280,128]{1,0:T(8,128)(2,1)} %refs_4_.3) | copy-start | bytes 983044
  10.3 13.0 %collective-permute-start.46 = (f32[896,128]{1,0:T(8,128)S(1)}, f32[896,128]{1,0:T(8,128)S(1)}, u32[]{:S(2)}, u32[]{:S(2)}) collective-permute-start(f32[896,128]{1,0:T(8,128)S(1)} %get-tuple-element.416.refs_2_), channel_id=1, source_target_pairs={{0,1},{1,0},{2,3},{3,2},{4,5},{5,4},{6,7},{7,6},{8,9},{9,8},{10,11... | collective-permute-start | bytes 1376264 | tf_op jit(solution)/shard_map/ppermute | solution.py:504
  10.8 4.2 %collective-permute-start.18 = (f32[264,128]{1,0:T(8,128)S(1)}, f32[264,128]{1,0:T(8,128)}, u32[]{:S(2)}, u32[]{:S(2)}) collective-permute-start(f32[264,128]{1,0:T(8,128)S(1)} %param.18), channel_id=1, source_target_pairs={{0,8},{2,10},{4,12},{6,14},{8,0},{10,2},{12,4},{14,6},{16,24},{18,... | collective-permute-start | bytes 405512 | tf_op jit(solution)/shard_map/cond/branch_3_fun/ppermute | solution.py:504
  16.4 23.1 %collective-permute-start.47 = (f32[392,128]{1,0:T(8,128)S(1)}, f32[392,128]{1,0:T(8,128)S(1)}, u32[]{:S(2)}, u32[]{:S(2)}) collective-permute-start(f32[392,128]{1,0:T(8,128)S(1)} %get-tuple-element.424.refs_2_), channel_id=1, source_target_pairs={{0,1},{1,0},{2,3},{3,2},{4,5},{5,4},{6,7},{7,6},{8,9},{9,8},{10,11... | collective-permute-start | bytes 602120 | tf_op jit(solution)/shard_map/ppermute | solution.py:504
  24.6 16.4 %collective-permute-start.48 = (f32[896,128]{1,0:T(8,128)S(1)}, f32[896,128]{1,0:T(8,128)S(1)}, u32[]{:S(2)}, u32[]{:S(2)}) collective-permute-start(f32[896,128]{1,0:T(8,128)S(1)} %get-tuple-element.429.refs_1_), channel_id=1, source_target_pairs={{0,1},{1,0},{2,3},{3,2},{4,5},{5,4},{6,7},{7,6},{8,9},{9,8},{10,11... | collective-permute-start | bytes 1376264 | tf_op jit(solution)/shard_map/ppermute | solution.py:504
  25.5 14.0 %collective-permute-start.38 = (f32[264,128]{1,0:T(8,128)S(1)}, f32[264,128]{1,0:T(8,128)}, u32[]{:S(2)}, u32[]{:S(2)}) collective-permute-start(f32[264,128]{1,0:T(8,128)S(1)} %param.38), channel_id=1, source_target_pairs={{0,18},{2,16},{4,22},{6,20},{8,26},{10,24},{12,30},{14,28},{16,2},... | collective-permute-start | bytes 405512 | tf_op jit(solution)/shard_map/cond/branch_8_fun/ppermute | solution.py:504
  40.9 7.3 %collective-permute-start.54 = (f32[392,128]{1,0:T(8,128)S(1)}, f32[392,128]{1,0:T(8,128)S(1)}, u32[]{:S(2)}, u32[]{:S(2)}) collective-permute-start(f32[392,128]{1,0:T(8,128)S(1)} %get-tuple-element.443.refs_0_), channel_id=1, source_target_pairs={{0,1},{1,0},{2,3},{3,2},{4,5},{5,4},{6,7},{7,6},{8,9},{9,8},{10,11... | collective-permute-start | bytes 602120 | tf_op jit(solution)/shard_map/ppermute | solution.py:504
  42.3 12.5 %collective-permute-start.51 = (f32[264,128]{1,0:T(8,128)S(1)}, f32[264,128]{1,0:T(8,128)S(1)}, u32[]{:S(2)}, u32[]{:S(2)}) collective-permute-start(f32[264,128]{1,0:T(8,128)S(1)} %get-tuple-element.440), channel_id=1, source_target_pairs={{0,30},{2,28},{4,26},{6,24},{8,22},{10,20},{12,18},{14,16},{16,14}... | collective-permute-start | bytes 405512 | tf_op jit(solution)/shard_map/ppermute | solution.py:504
  45.5 5.6 %collective-permute-start.53 = (f32[256,128]{1,0:T(8,128)S(1)}, f32[256,128]{1,0:T(8,128)S(1)}, u32[]{:S(2)}, u32[]{:S(2)}) collective-permute-start(f32[256,128]{1,0:T(8,128)S(1)} %get-tuple-element.442.refs_0_), channel_id=1, source_target_pairs={{0,1},{1,0},{2,3},{3,2},{4,5},{5,4},{6,7},{7,6},{8,9},{9,8},{10,11... | collective-permute-start | bytes 393224 | tf_op jit(solution)/shard_map/ppermute | solution.py:504
  46.7 7.1 %collective-permute-start.52 = (f32[256,128]{1,0:T(8,128)S(1)}, f32[256,128]{1,0:T(8,128)S(1)}, u32[]{:S(2)}, u32[]{:S(2)}) collective-permute-start(f32[256,128]{1,0:T(8,128)S(1)} %get-tuple-element.441.refs_0_), channel_id=1, source_target_pairs={{0,1},{1,0},{2,3},{3,2},{4,5},{5,4},{6,7},{7,6},{8,9},{9,8},{10,11... | collective-permute-start | bytes 393224 | tf_op jit(solution)/shard_map/ppermute | solution.py:504
  46.9 9.0 %collective-permute-start.50 = (f32[192,128]{1,0:T(8,128)S(1)}, f32[192,128]{1,0:T(8,128)S(1)}, u32[]{:S(2)}, u32[]{:S(2)}) collective-permute-start(f32[192,128]{1,0:T(8,128)S(1)} %get-tuple-element.439.refs_0_), channel_id=1, source_target_pairs={{0,1},{1,0},{2,3},{3,2},{4,5},{5,4},{6,7},{7,6},{8,9},{9,8},{10,11... | collective-permute-start | bytes 294920 | tf_op jit(solution)/shard_map/ppermute | solution.py:504
  48.2 9.4 %collective-permute-start.49 = (f32[192,128]{1,0:T(8,128)S(1)}, f32[192,128]{1,0:T(8,128)S(1)}, u32[]{:S(2)}, u32[]{:S(2)}) collective-permute-start(f32[192,128]{1,0:T(8,128)S(1)} %get-tuple-element.437.refs_0_), channel_id=1, source_target_pairs={{0,1},{1,0},{2,3},{3,2},{4,5},{5,4},{6,7},{7,6},{8,9},{9,8},{10,11... | collective-permute-start | bytes 294920 | tf_op jit(solution)/shard_map/ppermute | solution.py:504
where the time goes:
time: 58.6 us
  waiting for transfers between devices  21.4 us (37%)
  starting transfers between devices  20.1 us (34%)
  Pallas kernels  15.9 us (27%)
  between operations  0.92 us (2%)
    ppermute x13, waiting for transfers between devices, swapped(): lax.ppermute(value, axis, [(a, a ^ mask) for a in range(lax.axis_size(axi...  21.4 us
    ppermute x13, starting transfers between devices, swapped(): lax.ppermute(value, axis, [(a, a ^ mask) for a in range(lax.axis_size(axi...  20.1 us
    pallas_call x6, Pallas kernels, stratum_call(): pl.pallas_call(kernel, out_shape=[jax.ShapeDtypeStruct(*spec) for spec in...  7.49 us
    pallas_call x5, Pallas kernels, user_log_call(): pl.pallas_call(functools.partial(user_log_kernel, at=at, rows=rows, shp_a...  4.69 us
    pallas_call x1, Pallas kernels, start_call(): pl.pallas_call(start_kernel, out_shape=[pltpu.VMEM((8, depth), F32), pltp...  1.96 us
  transfers between devices with their start and end apart: 13, of which 8 were waited for; matrix products, arithmetic and copies ran while one was open for 0% of the time, Pallas kernels for 22%

commit v1 on v0

--- a/solution.py
+++ b/solution.py
@@ -16,7 +16,7 @@
 
 
 def chunk_rows(rows):
-    first = max(rows * 3 // 10 // START_TILE, 1) * START_TILE
+    first = max(rows // 2 // START_TILE, 1) * START_TILE
     return [first, rows - first] if first < rows else [rows]
 
 

time: 58.6 us -> 57.6 us (0.983)
  the two profiles are of different devices: /device:TPU:1 before, /device:TPU:0 now
where the time goes in v1:
time: 57.6 us; the launch traced here: 57.4 us
  starting transfers between devices  21.1 us (37%)
  waiting for transfers between devices  19.9 us (35%)
  Pallas kernels  15.2 us (26%)
  between operations  0.89 us (2%)
    ppermute x12, starting transfers between devices, swapped(): lax.ppermute(value, axis, [(a, a ^ mask) for a in range(lax.axis_size(axi...  21.1 us
    ppermute x12, waiting for transfers between devices, swapped(): lax.ppermute(value, axis, [(a, a ^ mask) for a in range(lax.axis_size(axi...  19.9 us
    pallas_call x6, Pallas kernels, stratum_call(): pl.pallas_call(kernel, out_shape=[jax.ShapeDtypeStruct(*spec) for spec in...  7.5 us
    pallas_call x4, Pallas kernels, user_log_call(): pl.pallas_call(functools.partial(user_log_kernel, at=at, rows=rows, shp_a...  3.96 us
    pallas_call x1, Pallas kernels, start_call(): pl.pallas_call(start_kernel, out_shape=[pltpu.VMEM((8, depth), F32), pltp...  1.96 us
  transfers between devices with their start and end apart: 12, of which 9 were waited for; matrix products, arithmetic and copies ran while one was open for 0% of the time, Pallas kernels for 22%

profile of v1, /device:TPU:0, one launch (start us, length us, event | category | flops | bytes accessed | tf_op | source)
XLA Modules:
  0.0 57.4 jit_solution(1226860180115670260)
XLA Ops:
  0.6 0.9 %prepare.1 = (f32[256,128]{1,0:T(8,128)S(1)}, s32[1]{0:T(128)S(4)}, s32[1]{0:T(128)S(4)}, s32[1]{0:T(128)S(4)}) custom-call(s32[3]{0:T(128)} %matchings_hbm.1, bf16[256,128]{1,0:T(8,128)(2,1)} %shape_hbm.1), custom_call_target="tpu_custom_call" | custom-call | tf_op jit(solution)/shard_map/prepare/pallas_call | solution.py:151
  1.5 8.6 %conditional.3 = (f32[8,128]{1,0:T(8,128)S(1)}, bf16[640,128]{1,0:T(8,128)(2,1)S(1)}, bf16[640,256]{1,0:T(8,128)(2,1)S(1)}, bf16[256,128]{1,0:T(8,128)(2,1)S(1)}...) conditional(s32[]{:T(128)} %bitcast, ...), branch_computations={%region_0.0_spmd, %region_1.0_spmd, %region_2.0_spmd, %region_3.0_... | conditional | flops 12589465600 | bytes 129179752 | solution.py:513
  1.6 3.5 %collective-permute-start.6 = (f32[256,128]{1,0:T(8,128)S(1)}, f32[256,128]{1,0:T(8,128)S(1)}, u32[]{:S(2)}, u32[]{:S(2)}) collective-permute-start(f32[256,128]{1,0:T(8,128)S(1)} %get-tuple-element.236), channel_id=1, source_target_pairs={{0,14},{2,12},{4,10},{6,8},{8,6},{10,4},{12,2},{14,0},{16,30},{18,... | collective-permute-start | bytes 393224 | tf_op jit(solution)/shard_map/cond/branch_6_fun/ppermute | solution.py:504
  5.1 2.0 %user_start.21 = (f32[8,128]{1,0:T(8,128)S(1)}, bf16[640,256]{1,0:T(8,128)(2,1)S(1)}, bf16[640,128]{1,0:T(8,128)(2,1)S(1)}, bf16[640,128]{1,0:T(8,128)(2,1)S(1)}) custom-call(bf16[1280,128]{1,0:T(8,128)(2,1)} %get-tuple-element.230.shape_hbm, bf16[3,1280,256]{2,1,0:T(8,128)(2,1)} %get-tuple-element.231.interactions.refs_1_), custom_call_target="tpu_custom_call" | custom-call | flops 6553600 | bytes 655360 | tf_op jit(solution)/shard_map/cond/branch_6_fun/user_start/pallas_call | solution.py:207
  7.0 1.9 %collective-permute-done.6.refs_3_ = f32[256,128]{1,0:T(8,128)S(1)} collective-permute-done((f32[256,128]{1,0:T(8,128)S(1)}, f32[256,128]{1,0:T(8,128)S(1)}, u32[]{:S(2)}, u32[]{:S(2)}) %collective-permute-start.6) | collective-permute-done | bytes 131104 | tf_op jit(solution)/shard_map/cond/branch_6_fun/ppermute | solution.py:504
  8.9 1.0 %stratum0_at0.21 = (f32[648,128]{1,0:T(8,128)S(1)}, bf16[256,128]{1,0:T(8,128)(2,1)S(1)}, f32[256,128]{1,0:T(8,128)S(1)}, bf16[640,256]{1,0:T(8,128)(2,1)S(1)}, ...) custom-call(bf16[640,256]{1,0:T(8,128)(2,1)S(1)} %get-tuple-element.234.refs_0_, ...), custom_call_target="tpu_custom_call" | custom-call | flops 12582912000 | bytes 128000000 | tf_op jit(solution)/shard_map/cond/branch_6_fun/stratum0_at0/pallas_call | solution.py:403
  10.1 2.2 %collective-permute-start.45 = (f32[648,128]{1,0:T(8,128)S(1)}, f32[648,128]{1,0:T(8,128)S(1)}, u32[]{:S(2)}, u32[]{:S(2)}) collective-permute-start(f32[648,128]{1,0:T(8,128)S(1)} %get-tuple-element.409.refs_2_), channel_id=1, source_target_pairs={{0,1},{1,0},{2,3},{3,2},{4,5},{5,4},{6,7},{7,6},{8,9},{9,8},{10,11... | collective-permute-start | bytes 995336 | tf_op jit(solution)/shard_map/ppermute | solution.py:504
  12.3 0.0 copy-start
  12.3 1.4 %stratum0_at640.1 = (f32[640,128]{1,0:T(8,128)S(1)}, f32[264,128]{1,0:T(8,128)S(1)}, bf16[640,256]{1,0:T(8,128)(2,1)S(1)}) custom-call(bf16[640,256]{1,0:T(8,128)(2,1)S(1)} %get-tuple-element.401.refs_0_, bf16[3,1280,256]{2,1,0:T(8,128)(2,1)} %refs_1_.7, bf16[640,128]{1,0:T(8,128)(2,1)S(1)} %get-tuple-element.402.refs_2_, ...), custom_call_target="tpu_custom_call" | custom-call | flops 12582912000 | bytes 128000000 | tf_op jit(solution)/shard_map/stratum0_at640/pallas_call | solution.py:403
  13.8 0.1 collective-permute-start.46
  13.9 9.2 %conditional.4 = (f32[264,128]{1,0:T(8,128)}) conditional(s32[]{:T(128)} %bitcast.1, f32[264,128]{1,0:T(8,128)S(1)} %get-tuple-element.411, f32[264,128]{1,0:T(8,128)S(1)} %get-tuple-element.411, f32[264,128]{1,0:T(8,128)S(1)} %get-tuple-element.411, f32[264,128]{1,0:T(8,128)S(1)} %get-tuple-element.411, ...), branch_computations={%region_15.0_spmd, %region_16.0_spmd, %region_17.0_spmd, %region_1... | conditional | bytes 540720 | solution.py:513
  13.9 2.2 %collective-permute-start.23 = (f32[264,128]{1,0:T(8,128)S(1)}, f32[264,128]{1,0:T(8,128)}, u32[]{:S(2)}, u32[]{:S(2)}) collective-permute-start(f32[264,128]{1,0:T(8,128)S(1)} %param.23), channel_id=1, source_target_pairs={{0,18},{2,16},{4,22},{6,20},{8,26},{10,24},{12,30},{14,28},{16,2},... | collective-permute-start | bytes 405512 | tf_op jit(solution)/shard_map/cond/branch_8_fun/ppermute | solution.py:504
  16.1 7.0 %collective-permute-done.23 = f32[264,128]{1,0:T(8,128)} collective-permute-done((f32[264,128]{1,0:T(8,128)S(1)}, f32[264,128]{1,0:T(8,128)}, u32[]{:S(2)}, u32[]{:S(2)}) %collective-permute-start.23) | collective-permute-done | bytes 135200 | tf_op jit(solution)/shard_map/cond/branch_8_fun/ppermute | solution.py:504
  23.1 0.0 collective-permute-done.45.refs_3_
  23.1 0.0 copy-done
  23.1 1.5 %stratum1_at0.1 = (f32[648,128]{1,0:T(8,128)S(1)}, f32[640,128]{1,0:T(8,128)S(1)}, f32[8,128]{1,0:T(8,128)S(1)}, bf16[256,128]{1,0:T(8,128)(2,1)S(1)}, f32[264,1...) custom-call(bf16[640,256]{1,0:T(8,128)(2,1)S(1)} %get-tuple-element., ...), custom_call_target="tpu_custom_call" | custom-call | flops 12582912000 | bytes 128000000 | tf_op jit(solution)/shard_map/stratum1_at0/pallas_call | solution.py:403
  24.6 2.4 %collective-permute-start.47 = (f32[648,128]{1,0:T(8,128)S(1)}, f32[648,128]{1,0:T(8,128)S(1)}, u32[]{:S(2)}, u32[]{:S(2)}) collective-permute-start(f32[648,128]{1,0:T(8,128)S(1)} %get-tuple-element.421.refs_2_), channel_id=1, source_target_pairs={{0,1},{1,0},{2,3},{3,2},{4,5},{5,4},{6,7},{7,6},{8,9},{9,8},{10,11... | collective-permute-start | bytes 995336 | tf_op jit(solution)/shard_map/ppermute | solution.py:504
  27.0 0.4 collective-permute-done.46.refs_3_
  27.4 1.0 %stratum1_at640.1 = (f32[640,128]{1,0:T(8,128)S(1)}, f32[640,128]{1,0:T(8,128)S(1)}, f32[264,128]{1,0:T(8,128)S(1)}, bf16[640,256]{1,0:T(8,128)(2,1)S(1)}) custom-call(bf16[640,256]{1,0:T(8,128)(2,1)S(1)} %get-tuple-element.412.refs_0_, bf16[3,1280,256]{2,1,0:T(8,128)(2,1)} %refs_1_.7, f32[640,128]{1,0:T(8,128)S(1)} %get-tuple-element.413.refs_2_, ...), custom_call_target="tpu_custom_call" | custom-call | flops 12582912000 | bytes 128000000 | tf_op jit(solution)/shard_map/stratum1_at640/pallas_call | solution.py:403
  28.5 1.8 %collective-permute-start.48 = (f32[640,128]{1,0:T(8,128)S(1)}, f32[640,128]{1,0:T(8,128)S(1)}, u32[]{:S(2)}, u32[]{:S(2)}) collective-permute-start(f32[640,128]{1,0:T(8,128)S(1)} %get-tuple-element.426.refs_1_), channel_id=1, source_target_pairs={{0,1},{1,0},{2,3},{3,2},{4,5},{5,4},{6,7},{7,6},{8,9},{9,8},{10,11... | collective-permute-start | bytes 983048 | tf_op jit(solution)/shard_map/ppermute | solution.py:504
  30.3 1.5 %conditional.5 = (f32[264,128]{1,0:T(8,128)}) conditional(s32[]{:T(128)} %bitcast.2, f32[264,128]{1,0:T(8,128)S(1)} %get-tuple-element.424, f32[264,128]{1,0:T(8,128)S(1)} %get-tuple-element.424, f32[264,128]{1,0:T(8,128)S(1)} %get-tuple-element.424, f32[264,128]{1,0:T(8,128)S(1)} %get-tuple-element.424, ...), branch_computations={%region_30.0_spmd, %region_31.0_spmd, %region_32.0_spmd, %region_3... | conditional | bytes 540720 | solution.py:513
  30.3 0.0 collective-permute-start.30
  30.3 1.5 %collective-permute-done.30 = f32[264,128]{1,0:T(8,128)} collective-permute-done((f32[264,128]{1,0:T(8,128)S(1)}, f32[264,128]{1,0:T(8,128)}, u32[]{:S(2)}, u32[]{:S(2)}) %collective-permute-start.30) | collective-permute-done | bytes 135200 | tf_op jit(solution)/shard_map/cond/branch_0_fun/ppermute | solution.py:504
  31.8 3.8 %collective-permute-done.47.refs_3_ = f32[648,128]{1,0:T(8,128)S(1)} collective-permute-done((f32[648,128]{1,0:T(8,128)S(1)}, f32[648,128]{1,0:T(8,128)S(1)}, u32[]{:S(2)}, u32[]{:S(2)}) %collective-permute-start.47) | collective-permute-done | bytes 331808 | tf_op jit(solution)/shard_map/ppermute | solution.py:504
  35.6 1.5 %stratum2_at0.1 = (f32[648,128]{1,0:T(8,128)S(1)}, f32[640,128]{1,0:T(8,128)S(1)}, f32[8,128]{1,0:T(8,128)S(1)}, bf16[256,128]{1,0:T(8,128)(2,1)S(1)}, f32[264,1...) custom-call(bf16[640,256]{1,0:T(8,128)(2,1)S(1)} %get-tuple-element., ...), custom_call_target="tpu_custom_call" | custom-call | flops 12582912000 | bytes 128000000 | tf_op jit(solution)/shard_map/stratum2_at0/pallas_call | solution.py:403
  37.1 2.1 %collective-permute-start.53 = (f32[648,128]{1,0:T(8,128)S(1)}, f32[648,128]{1,0:T(8,128)S(1)}, u32[]{:S(2)}, u32[]{:S(2)}) collective-permute-start(f32[648,128]{1,0:T(8,128)S(1)} %get-tuple-element.439.refs_0_), channel_id=1, source_target_pairs={{0,1},{1,0},{2,3},{3,2},{4,5},{5,4},{6,7},{7,6},{8,9},{9,8},{10,11... | collective-permute-start | bytes 995336 | tf_op jit(solution)/shard_map/ppermute | solution.py:504
  39.2 3.4 %collective-permute-done.48.refs_2_ = f32[640,128]{1,0:T(8,128)S(1)} collective-permute-done((f32[640,128]{1,0:T(8,128)S(1)}, f32[640,128]{1,0:T(8,128)S(1)}, u32[]{:S(2)}, u32[]{:S(2)}) %collective-permute-start.48) | collective-permute-done | bytes 327712 | tf_op jit(solution)/shard_map/ppermute | solution.py:504
  42.6 1.0 %stratum2_at640.1 = (f32[256,128]{1,0:T(8,128)S(1)}, f32[192,128]{1,0:T(8,128)S(1)}, f32[192,128]{1,0:T(8,128)S(1)}, f32[640,128]{1,0:T(8,128)S(1)}, f32[264,128]{1,0:T(8,128)S(1)}) custom-call(bf16[640,256]{1,0:T(8,128)(2,1)S(1)} %get-tuple-element.425.refs_0_, f32[640,128]{1,0:T(8,128)S(1)} %get-tuple-element.426.refs_1_, ...), custom_call_target="tpu_custom_call" | custom-call | flops 12582912000 | bytes 128000000 | tf_op jit(solution)/shard_map/stratum2_at640/pallas_call | solution.py:403
  43.6 3.2 %collective-permute-start.51 = (f32[264,128]{1,0:T(8,128)S(1)}, f32[264,128]{1,0:T(8,128)S(1)}, u32[]{:S(2)}, u32[]{:S(2)}) collective-permute-start(f32[264,128]{1,0:T(8,128)S(1)} %get-tuple-element.437), channel_id=1, source_target_pairs={{0,30},{2,28},{4,26},{6,24},{8,22},{10,20},{12,18},{14,16},{16,14}... | collective-permute-start | bytes 405512 | tf_op jit(solution)/shard_map/ppermute | solution.py:504
  46.9 1.5 %collective-permute-start.52 = (f32[256,128]{1,0:T(8,128)S(1)}, f32[256,128]{1,0:T(8,128)S(1)}, u32[]{:S(2)}, u32[]{:S(2)}) collective-permute-start(f32[256,128]{1,0:T(8,128)S(1)} %get-tuple-element.438.refs_0_), channel_id=1, source_target_pairs={{0,1},{1,0},{2,3},{3,2},{4,5},{5,4},{6,7},{7,6},{8,9},{9,8},{10,11... | collective-permute-start | bytes 393224 | tf_op jit(solution)/shard_map/ppermute | solution.py:504
  48.4 0.5 collective-permute-start.50
  48.9 1.5 %collective-permute-start.49 = (f32[192,128]{1,0:T(8,128)S(1)}, f32[192,128]{1,0:T(8,128)S(1)}, u32[]{:S(2)}, u32[]{:S(2)}) collective-permute-start(f32[192,128]{1,0:T(8,128)S(1)} %get-tuple-element.434.refs_0_), channel_id=1, source_target_pairs={{0,1},{1,0},{2,3},{3,2},{4,5},{5,4},{6,7},{7,6},{8,9},{9,8},{10,11... | collective-permute-start | bytes 294920 | tf_op jit(solution)/shard_map/ppermute | solution.py:504
  50.4 0.0 collective-permute-done.53.refs_1_
  50.4 1.3 %user_log_at0.1 = (bf16[1280,128]{1,0:T(8,128)(2,1)}, f32[8,128]{1,0:T(8,128)S(1)}) custom-call(f32[648,128]{1,0:T(8,128)S(1)} %get-tuple-element.439.refs_0_, f32[648,128]{1,0:T(8,128)S(1)} %collective-permute-done.53.refs_1_, f32[640,128]{1,0:T(8,128)S(1)} %get-tuple-element.440.refs_2_, f32[8,128]{1,0:T(8,128)S(1)} %get-tuple-element.428.refs_4_.refs_3_), custom_call_target="tpu_custom_call" | custom-call | flops 3276800 | bytes 1146880 | tf_op jit(solution)/shard_map/user_log_at0/pallas_call | solution.py:460
  51.7 0.4 collective-permute-done.52.refs_1_
  52.1 0.9 %user_log_at640.1 = (bf16[1280,128]{1,0:T(8,128)(2,1)}, f32[8,128]{1,0:T(8,128)S(1)}) custom-call(f32[256,128]{1,0:T(8,128)S(1)} %get-tuple-element.438.refs_0_, f32[256,128]{1,0:T(8,128)S(1)} %collective-permute-done.52.refs_1_, f32[640,128]{1,0:T(8,128)S(1)} %get-tuple-element.435.refs_2_, ...), custom_call_target="tpu_custom_call", output_to_operand_aliasing={{0}: (4, {})} | custom-call | flops 1310720 | bytes 458752 | tf_op jit(solution)/shard_map/user_log_at640/pallas_call | solution.py:460
  53.1 0.0 collective-permute-done.51.item
  53.1 0.9 %item_log.1 = (bf16[256,128]{1,0:T(8,128)(2,1)}, f32[8,128]{1,0:T(8,128)S(1)}) custom-call(f32[264,128]{1,0:T(8,128)S(1)} %collective-permute-done.51.item, f32[8,128]{1,0:T(8,128)S(1)} %get-tuple-element.443.through), custom_call_target="tpu_custom_call" | custom-call | flops 1310720 | bytes 196608 | tf_op jit(solution)/shard_map/item_log/pallas_call | solution.py:491
  54.0 0.2 collective-permute-done.50.refs_1_
  54.2 0.9 %user_log_at896.1 = (bf16[1280,128]{1,0:T(8,128)(2,1)}, f32[8,128]{1,0:T(8,128)S(1)}) custom-call(f32[192,128]{1,0:T(8,128)S(1)} %get-tuple-element.436.refs_0_, f32[192,128]{1,0:T(8,128)S(1)} %collective-permute-done.50.refs_1_, f32[640,128]{1,0:T(8,128)S(1)} %get-tuple-element.435.refs_2_, ...), custom_call_target="tpu_custom_call", output_to_operand_aliasing={{0}: (4, {})} | custom-call | flops 983040 | bytes 344064 | tf_op jit(solution)/shard_map/user_log_at896/pallas_call | solution.py:460
  55.1 1.2 %collective-permute-done.49.refs_1_ = f32[192,128]{1,0:T(8,128)S(1)} collective-permute-done((f32[192,128]{1,0:T(8,128)S(1)}, f32[192,128]{1,0:T(8,128)S(1)}, u32[]{:S(2)}, u32[]{:S(2)}) %collective-permute-start.49) | collective-permute-done | bytes 98336 | tf_op jit(solution)/shard_map/ppermute | solution.py:504
  56.3 0.9 %user_log_at1088.1 = bf16[1280,128]{1,0:T(8,128)(2,1)} custom-call(f32[192,128]{1,0:T(8,128)S(1)} %get-tuple-element.434.refs_0_, f32[192,128]{1,0:T(8,128)S(1)} %collective-permute-done.49.refs_1_, f32[640,128]{1,0:T(8,128)S(1)} %get-tuple-element.435.refs_2_, f32[8,128]{1,0:T(8,128)S(1)} %get-tuple-element.446.refs_3_, ...), custom_call_target="tpu_custom_call", output_to_operand_aliasing={{}: (4, {})} | custom-call | flops 983040 | bytes 344064 | tf_op jit(solution)/shard_map/user_log_at1088/pallas_call | solution.py:460
Async XLA Ops:
  1.6 7.4 %collective-permute-start.6 = (f32[256,128]{1,0:T(8,128)S(1)}, f32[256,128]{1,0:T(8,128)S(1)}, u32[]{:S(2)}, u32[]{:S(2)}) collective-permute-start(f32[256,128]{1,0:T(8,128)S(1)} %get-tuple-element.236), channel_id=1, source_target_pairs={{0,14},{2,12},{4,10},{6,8},{8,6},{10,4},{12,2},{14,0},{16,30},{18,... | collective-permute-start | bytes 393224 | tf_op jit(solution)/shard_map/cond/branch_6_fun/ppermute | solution.py:504
  10.1 13.0 %collective-permute-start.45 = (f32[648,128]{1,0:T(8,128)S(1)}, f32[648,128]{1,0:T(8,128)S(1)}, u32[]{:S(2)}, u32[]{:S(2)}) collective-permute-start(f32[648,128]{1,0:T(8,128)S(1)} %get-tuple-element.409.refs_2_), channel_id=1, source_target_pairs={{0,1},{1,0},{2,3},{3,2},{4,5},{5,4},{6,7},{7,6},{8,9},{9,8},{10,11... | collective-permute-start | bytes 995336 | tf_op jit(solution)/shard_map/ppermute | solution.py:504
  12.3 10.8 %copy-start = (bf16[1280,128]{1,0:T(8,128)(2,1)S(1)}, bf16[1280,128]{1,0:T(8,128)(2,1)}, u32[]{:S(2)}) copy-start(bf16[1280,128]{1,0:T(8,128)(2,1)} %refs_4_.3) | copy-start | bytes 983044
  13.8 13.7 %collective-permute-start.46 = (f32[640,128]{1,0:T(8,128)S(1)}, f32[640,128]{1,0:T(8,128)S(1)}, u32[]{:S(2)}, u32[]{:S(2)}) collective-permute-start(f32[640,128]{1,0:T(8,128)S(1)} %get-tuple-element.413.refs_2_), channel_id=1, source_target_pairs={{0,1},{1,0},{2,3},{3,2},{4,5},{5,4},{6,7},{7,6},{8,9},{9,8},{10,11... | collective-permute-start | bytes 983048 | tf_op jit(solution)/shard_map/ppermute | solution.py:504
  13.9 9.2 %collective-permute-start.23 = (f32[264,128]{1,0:T(8,128)S(1)}, f32[264,128]{1,0:T(8,128)}, u32[]{:S(2)}, u32[]{:S(2)}) collective-permute-start(f32[264,128]{1,0:T(8,128)S(1)} %param.23), channel_id=1, source_target_pairs={{0,18},{2,16},{4,22},{6,20},{8,26},{10,24},{12,30},{14,28},{16,2},... | collective-permute-start | bytes 405512 | tf_op jit(solution)/shard_map/cond/branch_8_fun/ppermute | solution.py:504
  24.6 10.9 %collective-permute-start.47 = (f32[648,128]{1,0:T(8,128)S(1)}, f32[648,128]{1,0:T(8,128)S(1)}, u32[]{:S(2)}, u32[]{:S(2)}) collective-permute-start(f32[648,128]{1,0:T(8,128)S(1)} %get-tuple-element.421.refs_2_), channel_id=1, source_target_pairs={{0,1},{1,0},{2,3},{3,2},{4,5},{5,4},{6,7},{7,6},{8,9},{9,8},{10,11... | collective-permute-start | bytes 995336 | tf_op jit(solution)/shard_map/ppermute | solution.py:504
  28.5 14.1 %collective-permute-start.48 = (f32[640,128]{1,0:T(8,128)S(1)}, f32[640,128]{1,0:T(8,128)S(1)}, u32[]{:S(2)}, u32[]{:S(2)}) collective-permute-start(f32[640,128]{1,0:T(8,128)S(1)} %get-tuple-element.426.refs_1_), channel_id=1, source_target_pairs={{0,1},{1,0},{2,3},{3,2},{4,5},{5,4},{6,7},{7,6},{8,9},{9,8},{10,11... | collective-permute-start | bytes 983048 | tf_op jit(solution)/shard_map/ppermute | solution.py:504
  30.3 1.5 %collective-permute-start.30 = (f32[264,128]{1,0:T(8,128)S(1)}, f32[264,128]{1,0:T(8,128)}, u32[]{:S(2)}, u32[]{:S(2)}) collective-permute-start(f32[264,128]{1,0:T(8,128)S(1)} %param.30), channel_id=1, source_target_pairs={{0,2},{2,0},{4,6},{6,4},{8,10},{10,8},{12,14},{14,12},{16,18},{18,... | collective-permute-start | bytes 405512 | tf_op jit(solution)/shard_map/cond/branch_0_fun/ppermute | solution.py:504
  37.1 13.3 %collective-permute-start.53 = (f32[648,128]{1,0:T(8,128)S(1)}, f32[648,128]{1,0:T(8,128)S(1)}, u32[]{:S(2)}, u32[]{:S(2)}) collective-permute-start(f32[648,128]{1,0:T(8,128)S(1)} %get-tuple-element.439.refs_0_), channel_id=1, source_target_pairs={{0,1},{1,0},{2,3},{3,2},{4,5},{5,4},{6,7},{7,6},{8,9},{9,8},{10,11... | collective-permute-start | bytes 995336 | tf_op jit(solution)/shard_map/ppermute | solution.py:504
  43.6 9.4 %collective-permute-start.51 = (f32[264,128]{1,0:T(8,128)S(1)}, f32[264,128]{1,0:T(8,128)S(1)}, u32[]{:S(2)}, u32[]{:S(2)}) collective-permute-start(f32[264,128]{1,0:T(8,128)S(1)} %get-tuple-element.437), channel_id=1, source_target_pairs={{0,30},{2,28},{4,26},{6,24},{8,22},{10,20},{12,18},{14,16},{16,14}... | collective-permute-start | bytes 405512 | tf_op jit(solution)/shard_map/ppermute | solution.py:504
  46.9 5.2 %collective-permute-start.52 = (f32[256,128]{1,0:T(8,128)S(1)}, f32[256,128]{1,0:T(8,128)S(1)}, u32[]{:S(2)}, u32[]{:S(2)}) collective-permute-start(f32[256,128]{1,0:T(8,128)S(1)} %get-tuple-element.438.refs_0_), channel_id=1, source_target_pairs={{0,1},{1,0},{2,3},{3,2},{4,5},{5,4},{6,7},{7,6},{8,9},{9,8},{10,11... | collective-permute-start | bytes 393224 | tf_op jit(solution)/shard_map/ppermute | solution.py:504
  48.4 5.8 %collective-permute-start.50 = (f32[192,128]{1,0:T(8,128)S(1)}, f32[192,128]{1,0:T(8,128)S(1)}, u32[]{:S(2)}, u32[]{:S(2)}) collective-permute-start(f32[192,128]{1,0:T(8,128)S(1)} %get-tuple-element.436.refs_0_), channel_id=1, source_target_pairs={{0,1},{1,0},{2,3},{3,2},{4,5},{5,4},{6,7},{7,6},{8,9},{9,8},{10,11... | collective-permute-start | bytes 294920 | tf_op jit(solution)/shard_map/ppermute | solution.py:504
  48.9 7.4 %collective-permute-start.49 = (f32[192,128]{1,0:T(8,128)S(1)}, f32[192,128]{1,0:T(8,128)S(1)}, u32[]{:S(2)}, u32[]{:S(2)}) collective-permute-start(f32[192,128]{1,0:T(8,128)S(1)} %get-tuple-element.434.refs_0_), channel_id=1, source_target_pairs={{0,1},{1,0},{2,3},{3,2},{4,5},{5,4},{6,7},{7,6},{8,9},{9,8},{10,11... | collective-permute-start | bytes 294920 | tf_op jit(solution)/shard_map/ppermute | solution.py:504

commit v2 on v1

--- a/solution.py
+++ b/solution.py
@@ -162,13 +162,16 @@
     return out[0], [choice[0] for choice in out[1:]]
 
 
-def start_kernel(shape_hbm, interactions, theta, counts, *refs):
-    uexps, (shape, sems) = refs[:-2], refs[-2:]
+def start_kernel(shape_hbm, interactions, theta, *refs, ahead):
+    counts, uexps, (shape, sems) = refs[:len(ahead)], refs[len(ahead):-2], refs[-2:]
     depth = shape.shape[1]
     load = pltpu.make_async_copy(shape_hbm, shape, sems.at[0])
-    ahead = pltpu.make_async_copy(interactions.at[0, pl.ds(0, counts.shape[0]), :], counts, sems.at[1])
     load.start()
-    ahead.start()
+    fetches = [
+        pltpu.make_async_copy(interactions.at[s, pl.ds(at, rows), :], counts[i], sems.at[i + 1])
+        for i, (s, at, rows) in enumerate(ahead)]
+    for fetch in fetches:
+        fetch.start()
     load.wait()
     total, low = jnp.zeros((8, depth), F32), jnp.ones((8, depth), F32)
     begin = 0
@@ -198,25 +201,27 @@
             redo_loop(uexp.shape[0], redo)
             begin += uexp.shape[0]
 
-    ahead.wait()
-
-
-def start_call(user_shape, interactions, sizes):
+    for fetch in fetches:
+        fetch.wait()
+
+
+def start_call(user_shape, interactions, sizes, ahead):
     rows, depth = user_shape.shape
     items = interactions.shape[2]
-    theta, counts, *uexps = pl.pallas_call(
-        start_kernel,
-        out_shape=[pltpu.VMEM((8, depth), F32), pltpu.VMEM((sizes[0], items), BF16)]
+    theta, *arrays = pl.pallas_call(
+        functools.partial(start_kernel, ahead=ahead),
+        out_shape=[pltpu.VMEM((8, depth), F32)]
+        + [pltpu.VMEM((fetch[2], items), BF16) for fetch in ahead]
         + [pltpu.VMEM((size, depth), BF16) for size in sizes],
         in_specs=[HBM_SPEC] * 2,
-        out_specs=[VMEM_SPEC] * (2 + len(sizes)),
-        scratch_shapes=[pltpu.VMEM((rows, depth), BF16), pltpu.SemaphoreType.DMA((2,))],
+        out_specs=[VMEM_SPEC] * (1 + len(ahead) + len(sizes)),
+        scratch_shapes=[pltpu.VMEM((rows, depth), BF16), pltpu.SemaphoreType.DMA((1 + len(ahead),))],
         compiler_params=PARAMS,
         cost_estimate=pl.CostEstimate(
             flops=40 * rows * depth, bytes_accessed=rows * depth * 4, transcendentals=2 * rows * depth),
         name="user_start",
     )(in_hbm(user_shape), in_hbm(interactions))
-    return theta, counts, uexps
+    return theta, arrays[:len(ahead)], arrays[len(ahead):]
 
 
 def dot_rows(a, b):
@@ -237,8 +242,8 @@
 
     if first and stratum > 0:
         fetch("item", ref["item"], ref["item_kept"])
-    if ahead:
-        fetch("ahead", ref["interactions"].at[ahead[0], pl.ds(ahead[1], ahead[2]), :], ref["counts_ahead"])
+    for i, (s, begin, size) in enumerate(ahead):
+        fetch(f"ahead{i}", ref["interactions"].at[s, pl.ds(begin, size), :], ref[f"counts_ahead{i}"])
     upart, counts, ratios, denominator = ref["upart0"], ref["counts"], ref["ratios"], ref["denominator"]
     uexp = ref["uexp"]
     extra = 8 if first else 0
@@ -359,8 +364,8 @@
                     redo_loop(rows if pair[0] is ratios else pair[0].shape[0], redo_stat)
                 update_items(total[...])
 
-    if ahead:
-        copies["ahead"].wait()
+    for i in range(len(ahead)):
+        copies[f"ahead{i}"].wait()
 
 
 def stratum_call(stratum, at, rows, items, depth, factor, first, last, earlier, cuts, ahead, operands):
@@ -381,11 +386,11 @@
         outs["uexp"] = ((rows, depth), BF16)
         if stratum > 0:
             outs["theta_new"] = ((8, depth), F32)
-    if ahead:
-        outs["counts_ahead"] = ((ahead[2], items), BF16)
+    for i, fetch in enumerate(ahead):
+        outs[f"counts_ahead{i}"] = ((fetch[2], items), BF16)
     scratch = {
         "denominator": pltpu.VMEM((rows, items), F32),
-        "sems": pltpu.SemaphoreType.DMA((2,)),
+        "sems": pltpu.SemaphoreType.DMA((1 + len(ahead),)),
     }
     if last:
         scratch["ratios"] = pltpu.VMEM((rows, items), BF16)
@@ -536,16 +541,20 @@
     item, choices = prepare_call(matchings, item_shape, group - 1)
     order = [(s, at, rows) for s in range(STRATA) for at, rows in zip(starts, sizes)]
 
+    def ahead_of(stratum):
+        begin = 0 if stratum == 0 else stratum * count + 1
+        return order[begin:(stratum + 1) * count + 1]
+
     def opening(arrived, user_shape, interactions):
-        theta, counts, uexps = start_call(user_shape, interactions, sizes)
-        operands = {"counts": counts, "interactions": interactions, "uexp_in": uexps[0], "item": arrived}
+        theta, counts, uexps = start_call(user_shape, interactions, sizes, ahead_of(0))
+        operands = {"counts": counts[0], "uexp_in": uexps[0], "item": arrived}
         if count == 1:
             operands["theta"] = theta
         out = stratum_call(
-            0, 0, sizes[0], items, depth, factor, True, count == 1, 0, sizes[:1], order[1], operands)
-        return theta, [out["uexp"], *uexps[1:]], out
-
-    theta, uexps, opened = moved(choices[0], item, opening, (user_shape, interactions))
+            0, 0, sizes[0], items, depth, factor, True, count == 1, 0, sizes[:1], [], operands)
+        return theta, [out["uexp"], *uexps[1:]], counts[1:], out
+
+    theta, uexps, fetched, opened = moved(choices[0], item, opening, (user_shape, interactions))
     rte = None
     shp = [None] * count
     sums = [None] * count
@@ -555,9 +564,11 @@
         for i, (at, rows) in enumerate(zip(starts, sizes)):
             first, last = i == 0, i == count - 1
             step = stratum * count + i
-            ahead = order[step + 1] if step + 1 < len(order) else None
+            ahead = ahead_of(stratum) if first and stratum > 0 else []
             cuts = last_cuts(rows) if step + 1 == len(order) else [rows]
-            operands = {"counts": counts} if step else {}
+            operands = {}
+            if step:
+                operands["counts"], fetched = fetched[0], fetched[1:]
             if ahead:
                 operands["interactions"] = interactions
             if stratum == 0:
@@ -587,7 +598,7 @@
             else:
                 out = stratum_call(
                     stratum, at, rows, items, depth, factor, first, last, i, cuts, ahead, operands)
-            counts = out.get("counts_ahead")
+            fetched = [*fetched, *(out[f"counts_ahead{n}"] for n in range(len(ahead)))]
             shp[i] = out.get("shp_new")
             sums[i] = exchanged(out["upart0"])
             if first:

time: 57.6 us -> 59.4 us (1.031)
  waiting for transfers between devices: 19.9 us -> 25 us
  starting transfers between devices: 21.1 us -> 19.4 us
  Pallas kernels: 15.2 us -> 14.1 us
    ppermute x12, waiting for transfers between devices: 19.9 us -> 25 us  [swapped(): lax.ppermute(value, axis, [(a, a ^ mask) for a in range(lax.axis_size(axi...]
    ppermute x12, starting transfers between devices: 21.1 us -> 19.4 us  [swapped(): lax.ppermute(value, axis, [(a, a ^ mask) for a in range(lax.axis_size(axi...]
    pallas_call x6, Pallas kernels: 7.5 us -> 6.33 us  [stratum_call(): pl.pallas_call(kernel, out_shape=[jax.ShapeDtypeStruct(*spec) for spec in...]
  transfers between devices with their start and end apart: 12 -> 12, of which waited for: 9 -> 9; matrix products, arithmetic and copies ran while one was open for 0% -> 0% of each run, Pallas kernels for 22% -> 20%
where the time goes in v2:
time: 59.4 us; the launch traced here: 59.6 us
  waiting for transfers between devices  25 us (42%)
  starting transfers between devices  19.4 us (33%)
  Pallas kernels  14.1 us (24%)
  between operations  0.89 us (1%)
    ppermute x12, waiting for transfers between devices, swapped(): lax.ppermute(value, axis, [(a, a ^ mask) for a in range(lax.axis_size(axi...  25 us
    ppermute x12, starting transfers between devices, swapped(): lax.ppermute(value, axis, [(a, a ^ mask) for a in range(lax.axis_size(axi...  19.4 us
    pallas_call x6, Pallas kernels, stratum_call(): pl.pallas_call(kernel, out_shape=[jax.ShapeDtypeStruct(*spec) for spec in...  6.33 us
    pallas_call x4, Pallas kernels, user_log_call(): pl.pallas_call(functools.partial(user_log_kernel, at=at, rows=rows, shp_a...  3.96 us
    pallas_call x1, Pallas kernels, start_call(): pl.pallas_call(functools.partial(start_kernel, ahead=ahead), out_shape=[p...  1.98 us
  transfers between devices with their start and end apart: 12, of which 9 were waited for; matrix products, arithmetic and copies ran while one was open for 0% of the time, Pallas kernels for 20%

profile of v2, /device:TPU:0, one launch (start us, length us, event | category | flops | bytes accessed | tf_op | source)
XLA Modules:
  0.0 59.6 jit_solution(12428370574452986172)
XLA Ops:
  0.6 0.9 %prepare.1 = (f32[256,128]{1,0:T(8,128)S(1)}, s32[1]{0:T(128)S(4)}, s32[1]{0:T(128)S(4)}, s32[1]{0:T(128)S(4)}) custom-call(s32[3]{0:T(128)} %matchings_hbm.1, bf16[256,128]{1,0:T(8,128)(2,1)} %shape_hbm.1), custom_call_target="tpu_custom_call" | custom-call | tf_op jit(solution)/shard_map/prepare/pallas_call | solution.py:151
  1.5 11.2 %conditional.3 = (f32[8,128]{1,0:T(8,128)S(1)}, bf16[640,128]{1,0:T(8,128)(2,1)S(1)}, bf16[640,256]{1,0:T(8,128)(2,1)S(1)}, bf16[640,256]{1,0:T(8,128)(2,1)S(1)}...) conditional(s32[]{:T(128)} %bitcast, ...), branch_computations={%region_0.0_spmd, %region_1.0_spmd, %region_2.0_spmd, %region_3.0_... | conditional | flops 12589465600 | bytes 129179760 | solution.py:518
  1.6 4.1 %collective-permute-start.7 = (f32[256,128]{1,0:T(8,128)S(1)}, f32[256,128]{1,0:T(8,128)S(1)}, u32[]{:S(2)}, u32[]{:S(2)}) collective-permute-start(f32[256,128]{1,0:T(8,128)S(1)} %get-tuple-element.258), channel_id=1, source_target_pairs={{0,16},{2,18},{4,20},{6,22},{8,24},{10,26},{12,28},{14,30},{16,0},... | collective-permute-start | bytes 393224 | tf_op jit(solution)/shard_map/cond/branch_7_fun/ppermute | solution.py:509
  5.7 2.0 %user_start.22 = (f32[8,128]{1,0:T(8,128)S(1)}, bf16[640,256]{1,0:T(8,128)(2,1)S(1)}, bf16[640,256]{1,0:T(8,128)(2,1)S(1)}, bf16[640,256]{1,0:T(8,128)(2,1)S(1)}...) custom-call(bf16[1280,128]{1,0:T(8,128)(2,1)} %get-tuple-element.250.shape_hbm, ...), custom_call_target="tpu_custom_call" | custom-call | flops 6553600 | bytes 655360 | tf_op jit(solution)/shard_map/cond/branch_7_fun/user_start/pallas_call | solution.py:211
  7.6 4.3 %collective-permute-done.7.refs_2_ = f32[256,128]{1,0:T(8,128)S(1)} collective-permute-done((f32[256,128]{1,0:T(8,128)S(1)}, f32[256,128]{1,0:T(8,128)S(1)}, u32[]{:S(2)}, u32[]{:S(2)}) %collective-permute-start.7) | collective-permute-done | bytes 131104 | tf_op jit(solution)/shard_map/cond/branch_7_fun/ppermute | solution.py:509
  12.0 0.6 stratum0_at0.22
  12.8 1.6 %collective-permute-start.45 = (f32[648,128]{1,0:T(8,128)S(1)}, f32[648,128]{1,0:T(8,128)S(1)}, u32[]{:S(2)}, u32[]{:S(2)}) collective-permute-start(f32[648,128]{1,0:T(8,128)S(1)} %get-tuple-element.417.refs_2_), channel_id=1, source_target_pairs={{0,1},{1,0},{2,3},{3,2},{4,5},{5,4},{6,7},{7,6},{8,9},{9,8},{10,11... | collective-permute-start | bytes 995336 | tf_op jit(solution)/shard_map/ppermute | solution.py:509
  14.4 0.0 copy-start
  14.4 0.6 %stratum0_at640.1 = (f32[640,128]{1,0:T(8,128)S(1)}, f32[264,128]{1,0:T(8,128)S(1)}) custom-call(bf16[640,256]{1,0:T(8,128)(2,1)S(1)} %get-tuple-element.419.refs_0_, bf16[640,128]{1,0:T(8,128)(2,1)S(1)} %get-tuple-element.420.refs_1_, f32[256,128]{1,0:T(8,128)S(1)} %get-tuple-element.421.refs_2_, bf16[256,128]{1,0:T(8,128)(2,1)S(1)} %get-tuple-element.422.refs_3_, ...), custom_call_target="tpu_custom_call" | custom-call | flops 12582912000 | bytes 128000000 | tf_op jit(solution)/shard_map/stratum0_at640/pallas_call | solution.py:408
  15.0 0.6 collective-permute-start.47
  15.6 9.2 %conditional.4 = (f32[264,128]{1,0:T(8,128)}) conditional(s32[]{:T(128)} %bitcast.1, f32[264,128]{1,0:T(8,128)S(1)} %get-tuple-element.426, f32[264,128]{1,0:T(8,128)S(1)} %get-tuple-element.426, f32[264,128]{1,0:T(8,128)S(1)} %get-tuple-element.426, f32[264,128]{1,0:T(8,128)S(1)} %get-tuple-element.426, ...), branch_computations={%region_15.0_spmd, %region_16.0_spmd, %region_17.0_spmd, %region_1... | conditional | bytes 540720 | solution.py:518
  15.6 0.9 %collective-permute-start.24 = (f32[264,128]{1,0:T(8,128)S(1)}, f32[264,128]{1,0:T(8,128)}, u32[]{:S(2)}, u32[]{:S(2)}) collective-permute-start(f32[264,128]{1,0:T(8,128)S(1)} %param.24), channel_id=1, source_target_pairs={{0,20},{2,22},{4,16},{6,18},{8,28},{10,30},{12,24},{14,26},{16,4},... | collective-permute-start | bytes 405512 | tf_op jit(solution)/shard_map/cond/branch_9_fun/ppermute | solution.py:509
  16.5 8.4 %collective-permute-done.24 = f32[264,128]{1,0:T(8,128)} collective-permute-done((f32[264,128]{1,0:T(8,128)S(1)}, f32[264,128]{1,0:T(8,128)}, u32[]{:S(2)}, u32[]{:S(2)}) %collective-permute-start.24) | collective-permute-done | bytes 135200 | tf_op jit(solution)/shard_map/cond/branch_9_fun/ppermute | solution.py:509
  24.8 0.0 collective-permute-done.45.refs_3_
  24.8 0.0 copy-done
  24.8 1.5 %stratum1_at0.1 = (f32[648,128]{1,0:T(8,128)S(1)}, f32[640,128]{1,0:T(8,128)S(1)}, f32[8,128]{1,0:T(8,128)S(1)}, bf16[256,128]{1,0:T(8,128)(2,1)S(1)}, f32[264,1...) custom-call(bf16[640,256]{1,0:T(8,128)(2,1)S(1)} %get-tuple-element., ...), custom_call_target="tpu_custom_call" | custom-call | flops 12582912000 | bytes 128000000 | tf_op jit(solution)/shard_map/stratum1_at0/pallas_call | solution.py:408
  26.4 1.6 %collective-permute-start.46 = (f32[648,128]{1,0:T(8,128)S(1)}, f32[648,128]{1,0:T(8,128)S(1)}, u32[]{:S(2)}, u32[]{:S(2)}) collective-permute-start(f32[648,128]{1,0:T(8,128)S(1)} %get-tuple-element.428.refs_2_), channel_id=1, source_target_pairs={{0,1},{1,0},{2,3},{3,2},{4,5},{5,4},{6,7},{7,6},{8,9},{9,8},{10,11... | collective-permute-start | bytes 995336 | tf_op jit(solution)/shard_map/ppermute | solution.py:509
  27.9 2.7 %collective-permute-done.47.refs_2_ = f32[640,128]{1,0:T(8,128)S(1)} collective-permute-done((f32[640,128]{1,0:T(8,128)S(1)}, f32[640,128]{1,0:T(8,128)S(1)}, u32[]{:S(2)}, u32[]{:S(2)}) %collective-permute-start.47) | collective-permute-done | bytes 327712 | tf_op jit(solution)/shard_map/ppermute | solution.py:509
  30.6 1.0 %stratum1_at640.1 = (f32[640,128]{1,0:T(8,128)S(1)}, f32[640,128]{1,0:T(8,128)S(1)}, f32[264,128]{1,0:T(8,128)S(1)}) custom-call(bf16[640,256]{1,0:T(8,128)(2,1)S(1)} %get-tuple-element.432.refs_0_, f32[640,128]{1,0:T(8,128)S(1)} %get-tuple-element.433.refs_1_, f32[640,128]{1,0:T(8,128)S(1)} %collective-permute-done.47.refs_2_, ...), custom_call_target="tpu_custom_call" | custom-call | flops 12582912000 | bytes 128000000 | tf_op jit(solution)/shard_map/stratum1_at640/pallas_call | solution.py:408
  31.6 1.6 %collective-permute-start.48 = (f32[640,128]{1,0:T(8,128)S(1)}, f32[640,128]{1,0:T(8,128)S(1)}, u32[]{:S(2)}, u32[]{:S(2)}) collective-permute-start(f32[640,128]{1,0:T(8,128)S(1)} %get-tuple-element.441.refs_1_), channel_id=1, source_target_pairs={{0,1},{1,0},{2,3},{3,2},{4,5},{5,4},{6,7},{7,6},{8,9},{9,8},{10,11... | collective-permute-start | bytes 983048 | tf_op jit(solution)/shard_map/ppermute | solution.py:509
  33.2 7.6 %conditional.5 = (f32[264,128]{1,0:T(8,128)}) conditional(s32[]{:T(128)} %bitcast.2, f32[264,128]{1,0:T(8,128)S(1)} %get-tuple-element.439, f32[264,128]{1,0:T(8,128)S(1)} %get-tuple-element.439, f32[264,128]{1,0:T(8,128)S(1)} %get-tuple-element.439, f32[264,128]{1,0:T(8,128)S(1)} %get-tuple-element.439, ...), branch_computations={%region_30.0_spmd, %region_31.0_spmd, %region_32.0_spmd, %region_3... | conditional | bytes 540720 | solution.py:518
  33.2 1.0 %collective-permute-start.42 = (f32[264,128]{1,0:T(8,128)S(1)}, f32[264,128]{1,0:T(8,128)}, u32[]{:S(2)}, u32[]{:S(2)}) collective-permute-start(f32[264,128]{1,0:T(8,128)S(1)} %param.42), channel_id=1, source_target_pairs={{0,26},{2,24},{4,30},{6,28},{8,18},{10,16},{12,22},{14,20},{16,10}... | collective-permute-start | bytes 405512 | tf_op jit(solution)/shard_map/cond/branch_12_fun/ppermute | solution.py:509
  34.2 6.6 %collective-permute-done.42 = f32[264,128]{1,0:T(8,128)} collective-permute-done((f32[264,128]{1,0:T(8,128)S(1)}, f32[264,128]{1,0:T(8,128)}, u32[]{:S(2)}, u32[]{:S(2)}) %collective-permute-start.42) | collective-permute-done | bytes 135200 | tf_op jit(solution)/shard_map/cond/branch_12_fun/ppermute | solution.py:509
  40.9 0.0 collective-permute-done.46.refs_3_
  40.9 1.5 %stratum2_at0.1 = (f32[648,128]{1,0:T(8,128)S(1)}, f32[640,128]{1,0:T(8,128)S(1)}, f32[8,128]{1,0:T(8,128)S(1)}, bf16[256,128]{1,0:T(8,128)(2,1)S(1)}, f32[264,1...) custom-call(bf16[640,256]{1,0:T(8,128)(2,1)S(1)} %get-tuple-element., ...), custom_call_target="tpu_custom_call" | custom-call | flops 12582912000 | bytes 128000000 | tf_op jit(solution)/shard_map/stratum2_at0/pallas_call | solution.py:408
  42.4 0.5 collective-permute-start.53
  42.9 0.1 collective-permute-done.48.refs_2_
  43.0 1.0 %stratum2_at640.1 = (f32[256,128]{1,0:T(8,128)S(1)}, f32[192,128]{1,0:T(8,128)S(1)}, f32[192,128]{1,0:T(8,128)S(1)}, f32[640,128]{1,0:T(8,128)S(1)}, f32[264,128]{1,0:T(8,128)S(1)}) custom-call(bf16[640,256]{1,0:T(8,128)(2,1)S(1)} %get-tuple-element.440.refs_0_, f32[640,128]{1,0:T(8,128)S(1)} %get-tuple-element.441.refs_1_, ...), custom_call_target="tpu_custom_call" | custom-call | flops 12582912000 | bytes 128000000 | tf_op jit(solution)/shard_map/stratum2_at640/pallas_call | solution.py:408
  44.0 4.1 %collective-permute-start.51 = (f32[264,128]{1,0:T(8,128)S(1)}, f32[264,128]{1,0:T(8,128)S(1)}, u32[]{:S(2)}, u32[]{:S(2)}) collective-permute-start(f32[264,128]{1,0:T(8,128)S(1)} %get-tuple-element.452), channel_id=1, source_target_pairs={{0,30},{2,28},{4,26},{6,24},{8,22},{10,20},{12,18},{14,16},{16,14}... | collective-permute-start | bytes 405512 | tf_op jit(solution)/shard_map/ppermute | solution.py:509
  48.1 1.5 %collective-permute-start.52 = (f32[256,128]{1,0:T(8,128)S(1)}, f32[256,128]{1,0:T(8,128)S(1)}, u32[]{:S(2)}, u32[]{:S(2)}) collective-permute-start(f32[256,128]{1,0:T(8,128)S(1)} %get-tuple-element.453.refs_0_), channel_id=1, source_target_pairs={{0,1},{1,0},{2,3},{3,2},{4,5},{5,4},{6,7},{7,6},{8,9},{9,8},{10,11... | collective-permute-start | bytes 393224 | tf_op jit(solution)/shard_map/ppermute | solution.py:509
  49.6 0.5 collective-permute-start.50
  50.1 1.5 %collective-permute-start.49 = (f32[192,128]{1,0:T(8,128)S(1)}, f32[192,128]{1,0:T(8,128)S(1)}, u32[]{:S(2)}, u32[]{:S(2)}) collective-permute-start(f32[192,128]{1,0:T(8,128)S(1)} %get-tuple-element.449.refs_0_), channel_id=1, source_target_pairs={{0,1},{1,0},{2,3},{3,2},{4,5},{5,4},{6,7},{7,6},{8,9},{9,8},{10,11... | collective-permute-start | bytes 294920 | tf_op jit(solution)/shard_map/ppermute | solution.py:509
  51.6 0.7 %collective-permute-done.53.refs_1_ = f32[648,128]{1,0:T(8,128)S(1)} collective-permute-done((f32[648,128]{1,0:T(8,128)S(1)}, f32[648,128]{1,0:T(8,128)S(1)}, u32[]{:S(2)}, u32[]{:S(2)}) %collective-permute-start.53) | collective-permute-done | bytes 331808 | tf_op jit(solution)/shard_map/ppermute | solution.py:509
  52.3 1.3 %user_log_at0.1 = (bf16[1280,128]{1,0:T(8,128)(2,1)}, f32[8,128]{1,0:T(8,128)S(1)}) custom-call(f32[648,128]{1,0:T(8,128)S(1)} %get-tuple-element.454.refs_0_, f32[648,128]{1,0:T(8,128)S(1)} %collective-permute-done.53.refs_1_, f32[640,128]{1,0:T(8,128)S(1)} %get-tuple-element.455.refs_2_, f32[8,128]{1,0:T(8,128)S(1)} %get-tuple-element.443.refs_4_.refs_3_), custom_call_target="tpu_custom_call" | custom-call | flops 3276800 | bytes 1146880 | tf_op jit(solution)/shard_map/user_log_at0/pallas_call | solution.py:465
  53.5 0.8 %collective-permute-done.52.refs_1_ = f32[256,128]{1,0:T(8,128)S(1)} collective-permute-done((f32[256,128]{1,0:T(8,128)S(1)}, f32[256,128]{1,0:T(8,128)S(1)}, u32[]{:S(2)}, u32[]{:S(2)}) %collective-permute-start.52) | collective-permute-done | bytes 131104 | tf_op jit(solution)/shard_map/ppermute | solution.py:509
  54.3 0.9 %user_log_at640.1 = (bf16[1280,128]{1,0:T(8,128)(2,1)}, f32[8,128]{1,0:T(8,128)S(1)}) custom-call(f32[256,128]{1,0:T(8,128)S(1)} %get-tuple-element.453.refs_0_, f32[256,128]{1,0:T(8,128)S(1)} %collective-permute-done.52.refs_1_, f32[640,128]{1,0:T(8,128)S(1)} %get-tuple-element.450.refs_2_, ...), custom_call_target="tpu_custom_call", output_to_operand_aliasing={{0}: (4, {})} | custom-call | flops 1310720 | bytes 458752 | tf_op jit(solution)/shard_map/user_log_at640/pallas_call | solution.py:465
  55.3 0.0 collective-permute-done.51.item
  55.3 0.9 %item_log.1 = (bf16[256,128]{1,0:T(8,128)(2,1)}, f32[8,128]{1,0:T(8,128)S(1)}) custom-call(f32[264,128]{1,0:T(8,128)S(1)} %collective-permute-done.51.item, f32[8,128]{1,0:T(8,128)S(1)} %get-tuple-element.458.through), custom_call_target="tpu_custom_call" | custom-call | flops 1310720 | bytes 196608 | tf_op jit(solution)/shard_map/item_log/pallas_call | solution.py:496
  56.2 0.2 collective-permute-done.50.refs_1_
  56.4 0.9 %user_log_at896.1 = (bf16[1280,128]{1,0:T(8,128)(2,1)}, f32[8,128]{1,0:T(8,128)S(1)}) custom-call(f32[192,128]{1,0:T(8,128)S(1)} %get-tuple-element.451.refs_0_, f32[192,128]{1,0:T(8,128)S(1)} %collective-permute-done.50.refs_1_, f32[640,128]{1,0:T(8,128)S(1)} %get-tuple-element.450.refs_2_, ...), custom_call_target="tpu_custom_call", output_to_operand_aliasing={{0}: (4, {})} | custom-call | flops 983040 | bytes 344064 | tf_op jit(solution)/shard_map/user_log_at896/pallas_call | solution.py:465
  57.3 1.2 %collective-permute-done.49.refs_1_ = f32[192,128]{1,0:T(8,128)S(1)} collective-permute-done((f32[192,128]{1,0:T(8,128)S(1)}, f32[192,128]{1,0:T(8,128)S(1)}, u32[]{:S(2)}, u32[]{:S(2)}) %collective-permute-start.49) | collective-permute-done | bytes 98336 | tf_op jit(solution)/shard_map/ppermute | solution.py:509
  58.5 0.9 %user_log_at1088.1 = bf16[1280,128]{1,0:T(8,128)(2,1)} custom-call(f32[192,128]{1,0:T(8,128)S(1)} %get-tuple-element.449.refs_0_, f32[192,128]{1,0:T(8,128)S(1)} %collective-permute-done.49.refs_1_, f32[640,128]{1,0:T(8,128)S(1)} %get-tuple-element.450.refs_2_, f32[8,128]{1,0:T(8,128)S(1)} %get-tuple-element.461.refs_3_, ...), custom_call_target="tpu_custom_call", output_to_operand_aliasing={{}: (4, {})} | custom-call | flops 983040 | bytes 344064 | tf_op jit(solution)/shard_map/user_log_at1088/pallas_call | solution.py:465
Async XLA Ops:
  1.6 10.4 %collective-permute-start.7 = (f32[256,128]{1,0:T(8,128)S(1)}, f32[256,128]{1,0:T(8,128)S(1)}, u32[]{:S(2)}, u32[]{:S(2)}) collective-permute-start(f32[256,128]{1,0:T(8,128)S(1)} %get-tuple-element.258), channel_id=1, source_target_pairs={{0,16},{2,18},{4,20},{6,22},{8,24},{10,26},{12,28},{14,30},{16,0},... | collective-permute-start | bytes 393224 | tf_op jit(solution)/shard_map/cond/branch_7_fun/ppermute | solution.py:509
  12.8 12.1 %collective-permute-start.45 = (f32[648,128]{1,0:T(8,128)S(1)}, f32[648,128]{1,0:T(8,128)S(1)}, u32[]{:S(2)}, u32[]{:S(2)}) collective-permute-start(f32[648,128]{1,0:T(8,128)S(1)} %get-tuple-element.417.refs_2_), channel_id=1, source_target_pairs={{0,1},{1,0},{2,3},{3,2},{4,5},{5,4},{6,7},{7,6},{8,9},{9,8},{10,11... | collective-permute-start | bytes 995336 | tf_op jit(solution)/shard_map/ppermute | solution.py:509
  14.4 10.5 %copy-start = (bf16[1280,128]{1,0:T(8,128)(2,1)S(1)}, bf16[1280,128]{1,0:T(8,128)(2,1)}, u32[]{:S(2)}) copy-start(bf16[1280,128]{1,0:T(8,128)(2,1)} %refs_3_.1) | copy-start | bytes 983044
  15.0 15.6 %collective-permute-start.47 = (f32[640,128]{1,0:T(8,128)S(1)}, f32[640,128]{1,0:T(8,128)S(1)}, u32[]{:S(2)}, u32[]{:S(2)}) collective-permute-start(f32[640,128]{1,0:T(8,128)S(1)} %get-tuple-element.433.refs_1_), channel_id=1, source_target_pairs={{0,1},{1,0},{2,3},{3,2},{4,5},{5,4},{6,7},{7,6},{8,9},{9,8},{10,11... | collective-permute-start | bytes 983048 | tf_op jit(solution)/shard_map/ppermute | solution.py:509
  15.6 9.2 %collective-permute-start.24 = (f32[264,128]{1,0:T(8,128)S(1)}, f32[264,128]{1,0:T(8,128)}, u32[]{:S(2)}, u32[]{:S(2)}) collective-permute-start(f32[264,128]{1,0:T(8,128)S(1)} %param.24), channel_id=1, source_target_pairs={{0,20},{2,22},{4,16},{6,18},{8,28},{10,30},{12,24},{14,26},{16,4},... | collective-permute-start | bytes 405512 | tf_op jit(solution)/shard_map/cond/branch_9_fun/ppermute | solution.py:509
  26.4 14.5 %collective-permute-start.46 = (f32[648,128]{1,0:T(8,128)S(1)}, f32[648,128]{1,0:T(8,128)S(1)}, u32[]{:S(2)}, u32[]{:S(2)}) collective-permute-start(f32[648,128]{1,0:T(8,128)S(1)} %get-tuple-element.428.refs_2_), channel_id=1, source_target_pairs={{0,1},{1,0},{2,3},{3,2},{4,5},{5,4},{6,7},{7,6},{8,9},{9,8},{10,11... | collective-permute-start | bytes 995336 | tf_op jit(solution)/shard_map/ppermute | solution.py:509
  31.6 11.3 %collective-permute-start.48 = (f32[640,128]{1,0:T(8,128)S(1)}, f32[640,128]{1,0:T(8,128)S(1)}, u32[]{:S(2)}, u32[]{:S(2)}) collective-permute-start(f32[640,128]{1,0:T(8,128)S(1)} %get-tuple-element.441.refs_1_), channel_id=1, source_target_pairs={{0,1},{1,0},{2,3},{3,2},{4,5},{5,4},{6,7},{7,6},{8,9},{9,8},{10,11... | collective-permute-start | bytes 983048 | tf_op jit(solution)/shard_map/ppermute | solution.py:509
  33.2 7.6 %collective-permute-start.42 = (f32[264,128]{1,0:T(8,128)S(1)}, f32[264,128]{1,0:T(8,128)}, u32[]{:S(2)}, u32[]{:S(2)}) collective-permute-start(f32[264,128]{1,0:T(8,128)S(1)} %param.42), channel_id=1, source_target_pairs={{0,26},{2,24},{4,30},{6,28},{8,18},{10,16},{12,22},{14,20},{16,10}... | collective-permute-start | bytes 405512 | tf_op jit(solution)/shard_map/cond/branch_12_fun/ppermute | solution.py:509
  42.4 9.9 %collective-permute-start.53 = (f32[648,128]{1,0:T(8,128)S(1)}, f32[648,128]{1,0:T(8,128)S(1)}, u32[]{:S(2)}, u32[]{:S(2)}) collective-permute-start(f32[648,128]{1,0:T(8,128)S(1)} %get-tuple-element.454.refs_0_), channel_id=1, source_target_pairs={{0,1},{1,0},{2,3},{3,2},{4,5},{5,4},{6,7},{7,6},{8,9},{9,8},{10,11... | collective-permute-start | bytes 995336 | tf_op jit(solution)/shard_map/ppermute | solution.py:509
  44.0 11.3 %collective-permute-start.51 = (f32[264,128]{1,0:T(8,128)S(1)}, f32[264,128]{1,0:T(8,128)S(1)}, u32[]{:S(2)}, u32[]{:S(2)}) collective-permute-start(f32[264,128]{1,0:T(8,128)S(1)} %get-tuple-element.452), channel_id=1, source_target_pairs={{0,30},{2,28},{4,26},{6,24},{8,22},{10,20},{12,18},{14,16},{16,14}... | collective-permute-start | bytes 405512 | tf_op jit(solution)/shard_map/ppermute | solution.py:509
  48.1 6.2 %collective-permute-start.52 = (f32[256,128]{1,0:T(8,128)S(1)}, f32[256,128]{1,0:T(8,128)S(1)}, u32[]{:S(2)}, u32[]{:S(2)}) collective-permute-start(f32[256,128]{1,0:T(8,128)S(1)} %get-tuple-element.453.refs_0_), channel_id=1, source_target_pairs={{0,1},{1,0},{2,3},{3,2},{4,5},{5,4},{6,7},{7,6},{8,9},{9,8},{10,11... | collective-permute-start | bytes 393224 | tf_op jit(solution)/shard_map/ppermute | solution.py:509
  49.6 6.9 %collective-permute-start.50 = (f32[192,128]{1,0:T(8,128)S(1)}, f32[192,128]{1,0:T(8,128)S(1)}, u32[]{:S(2)}, u32[]{:S(2)}) collective-permute-start(f32[192,128]{1,0:T(8,128)S(1)} %get-tuple-element.451.refs_0_), channel_id=1, source_target_pairs={{0,1},{1,0},{2,3},{3,2},{4,5},{5,4},{6,7},{7,6},{8,9},{9,8},{10,11... | collective-permute-start | bytes 294920 | tf_op jit(solution)/shard_map/ppermute | solution.py:509
  50.1 8.4 %collective-permute-start.49 = (f32[192,128]{1,0:T(8,128)S(1)}, f32[192,128]{1,0:T(8,128)S(1)}, u32[]{:S(2)}, u32[]{:S(2)}) collective-permute-start(f32[192,128]{1,0:T(8,128)S(1)} %get-tuple-element.449.refs_0_), channel_id=1, source_target_pairs={{0,1},{1,0},{2,3},{3,2},{4,5},{5,4},{6,7},{7,6},{8,9},{9,8},{10,11... | collective-permute-start | bytes 294920 | tf_op jit(solution)/shard_map/ppermute | solution.py:509

commit v3 on v2

--- a/solution.py
+++ b/solution.py
@@ -240,8 +240,6 @@
         copies[name] = pltpu.make_async_copy(source, target, ref["sems"].at[len(copies)])
         copies[name].start()
 
-    if first and stratum > 0:
-        fetch("item", ref["item"], ref["item_kept"])
     for i, (s, begin, size) in enumerate(ahead):
         fetch(f"ahead{i}", ref["interactions"].at[s, pl.ds(begin, size), :], ref[f"counts_ahead{i}"])
     upart, counts, ratios, denominator = ref["upart0"], ref["counts"], ref["ratios"], ref["denominator"]
@@ -277,22 +275,21 @@
     elif last:
         total_mean = ref["theta"]
 
-    if first and stratum > 0:
-        copies["item"].wait()
-    elif first:
+    meets = first and stratum == 0
+    item_exp_ref = ref["item_exp_new" if meets else "item_exp"]
+    if first or last:
+        item_rte = None if stratum == 0 else item[items:items + 8, :]
+    if first and not meets:
+        upart[0:8, :] = ref["item_sums"][...]
+    if meets:
         item[...] = ref["item"][...]
         uexp[...] = ref["uexp_in"][...]
-    if first or last:
-        item_rte = None if stratum == 0 else item[items:items + 8, :]
-    if first:
         item_exp, sums, low = exp_tile(item[0:items, :], item_rte, False)
         ref["item_exp_new"][...] = item_exp
         upart[0:8, :] = sums
         lows.append(low)
-        if item_rte is not None:
-            lows.append(usual(item_rte))
     else:
-        item_exp = ref["item_exp"][...]
+        item_exp = item_exp_ref[...]
 
     denominator[...] = dot_rows(uexp[...], item_exp)
     for t, step in tiles(rows):
@@ -308,7 +305,7 @@
 
     def update_items(istat):
         old = 1.0 if item_rte is None else item_rte
-        kept = ref["item_exp_new" if first else "item_exp"][...].astype(F32)
+        kept = item_exp_ref[...].astype(F32)
         ref["item_new"][0:items, :] = 0.5 * item[0:items, :] + 0.5 * (0.3 + factor * (kept * istat))
         ref["item_new"][items:items + 8, :] = 0.5 * old + 0.5 * (0.3 + factor * row_sum(total_mean[...]))
 
@@ -332,7 +329,7 @@
 
                 start = jnp.zeros_like(rte) if first else ref["theta"][...]
                 total_mean[...] = redo_loop(rows, redo_users, start)
-            if first:
+            if meets:
 
                 def redo_items(at, size, total):
                     place = pl.ds(at, size)
@@ -340,7 +337,7 @@
                     return total + part
 
                 upart[0:8, :] = redo_loop(items, redo_items, jnp.zeros((8, upart.shape[1]), F32))
-            kept = ref["item_exp_new" if first else "item_exp"]
+            kept = item_exp_ref
             for target, begin, skip, length in parts:
 
                 def redo_sums(at, size, _, target=target, begin=begin, skip=skip):
@@ -375,9 +372,9 @@
         outs["shp_new"] = ((rows, depth), F32)
     if first and stratum > 0:
         outs["rte_new"] = ((8, depth), F32)
-    if first:
+    if first and stratum == 0:
         outs["item_exp_new"] = ((items, depth), BF16)
-    if first:
+    if first and stratum == 0:
         outs["item_kept"] = (operands["item"].shape, F32)
     if last:
         outs["item_new"] = ((items + 8, depth), F32)
@@ -397,7 +394,7 @@
         if stratum > 0:
             scratch["uexp"] = pltpu.VMEM((rows, depth), BF16)
             scratch["theta_new"] = pltpu.VMEM((8, depth), F32)
-    hbm = ("interactions", "item") if stratum > 0 else ("interactions",)
+    hbm = ("interactions",)
     operands = {
         name: in_hbm(x) if name in hbm else in_vmem(x) if name in ("user_shape", "item") else x
         for name, x in operands.items()}
@@ -417,6 +414,45 @@
         name=f"stratum{stratum}_at{at}",
     )(*operands.values())
     return dict(zip(outs, results))
+
+
+def meet_kernel(item, kept, item_exp, sums, *, items):
+    rte = item[items:items + 8, :]
+    kept[items:items + 8, :] = rte
+
+    def step(i, carry):
+        place = pl.ds(pl.multiple_of(i * TILE, TILE), TILE)
+        x = item[place, :]
+        kept[place, :] = x
+        item_exp[place, :], part, low = exp_tile(x, rte, False)
+        return carry[0] + part, jnp.minimum(carry[1], low)
+
+    sums[...], low = lax.fori_loop(0, items // TILE, step, (jnp.zeros_like(rte), usual(rte)))
+
+    @pl.when(jnp.logical_not(above(low)))
+    def _():
+        def redo(at, size, total):
+            place = pl.ds(at, size)
+            item_exp[place, :], part, _ = exp_tile(item[place, :], rte, True)
+            return total + part
+
+        sums[...] = redo_loop(items, redo, jnp.zeros_like(rte))
+
+
+def meet_call(item):
+    rows, depth = item.shape
+    items = rows - 8
+    kept, item_exp, sums = pl.pallas_call(
+        functools.partial(meet_kernel, items=items),
+        out_shape=[pltpu.VMEM(item.shape, F32), pltpu.VMEM((items, depth), BF16), pltpu.VMEM((8, depth), F32)],
+        in_specs=[VMEM_SPEC],
+        out_specs=[VMEM_SPEC] * 3,
+        compiler_params=PARAMS,
+        cost_estimate=pl.CostEstimate(
+            flops=40 * items * depth, bytes_accessed=items * depth * 10, transcendentals=2 * items * depth),
+        name="meet_items",
+    )(in_vmem(item))
+    return {"item_kept": kept, "item_exp": item_exp, "item_sums": sums}
 
 
 def user_log_kernel(*refs, at, rows, shp_at, factor, first, filled):
@@ -559,7 +595,7 @@
     shp = [None] * count
     sums = [None] * count
     for stratum in range(STRATA):
-        carried = {"theta": theta}
+        carried = {"theta": theta} if stratum == 0 else {"theta": theta, **item}
         earlier = {}
         for i, (at, rows) in enumerate(zip(starts, sizes)):
             first, last = i == 0, i == count - 1
@@ -583,12 +619,12 @@
                     operands["rte"] = rte
                 elif stratum > 1:
                     operands["rte_old"] = rte
-            if first:
-                operands["item"] = item
-            elif last:
+            if step:
+                operands["item_exp"] = carried["item_exp"]
+            if step and (first or last):
                 operands["item_kept"] = carried["item_kept"]
-            if not first:
-                operands["item_exp"] = carried["item_exp"]
+            if step and first:
+                operands["item_sums"] = carried["item_sums"]
             if last:
                 operands.update(earlier)
             if (stratum > 0 and not first) or (stratum == 0 and last):
@@ -603,8 +639,8 @@
             sums[i] = exchanged(out["upart0"])
             if first:
                 rte = out.get("rte_new")
-                carried["item_exp"] = out["item_exp_new"]
-                carried["item_kept"] = out["item_kept"]
+                if stratum == 0:
+                    carried["item_exp"], carried["item_kept"] = out["item_exp_new"], out["item_kept"]
             if last:
                 item = out["item_new"]
             else:
@@ -612,7 +648,7 @@
                 if stratum > 0:
                     carried["theta"] = out["theta_new"]
         if stratum + 1 < STRATA:
-            item = moved(choices[stratum + 1], item)
+            item = moved(choices[stratum + 1], item, meet_call)
         else:
             item = swapped(item, "users", group - 1)
     user_log = None

time: 59.4 us -> 61.5 us (1.035)
  starting transfers between devices: 19.4 us -> 21 us
  Pallas kernels: 14.1 us -> 14.8 us
    ppermute x12, starting transfers between devices: 19.4 us -> 21 us  [swapped(): lax.ppermute(value, axis, [(a, a ^ mask) for a in range(lax.axis_size(axi...]
  transfers between devices with their start and end apart: 12 -> 12, of which waited for: 9 -> 8; matrix products, arithmetic and copies ran while one was open for 0% -> 0% of each run, Pallas kernels for 20% -> 20%
where the time goes in v3:
time: 61.5 us; the launch traced here: 61.6 us
  waiting for transfers between devices  24.6 us (40%)
  starting transfers between devices  21 us (34%)
  Pallas kernels  14.8 us (24%)
  between operations  0.94 us (2%)
    ppermute x12, waiting for transfers between devices, swapped(): lax.ppermute(value, axis, [(a, a ^ mask) for a in range(lax.axis_size(axi...  24.6 us
    ppermute x12, starting transfers between devices, swapped(): lax.ppermute(value, axis, [(a, a ^ mask) for a in range(lax.axis_size(axi...  21 us
    pallas_call x6, Pallas kernels, stratum_call(): pl.pallas_call(kernel, out_shape=[jax.ShapeDtypeStruct(*spec) for spec in...  6.42 us
    pallas_call x4, Pallas kernels, user_log_call(): pl.pallas_call(functools.partial(user_log_kernel, at=at, rows=rows, shp_a...  3.97 us
    pallas_call x1, Pallas kernels, start_call(): pl.pallas_call(functools.partial(start_kernel, ahead=ahead), out_shape=[p...  1.98 us
  transfers between devices with their start and end apart: 12, of which 8 were waited for; matrix products, arithmetic and copies ran while one was open for 0% of the time, Pallas kernels for 20%

profile of v3, /device:TPU:0, one launch (start us, length us, event | category | flops | bytes accessed | tf_op | source)
XLA Modules:
  0.0 61.6 jit_solution(16169342992639354735)
XLA Ops:
  0.6 0.9 %prepare.1 = (f32[256,128]{1,0:T(8,128)S(1)}, s32[1]{0:T(128)S(4)}, s32[1]{0:T(128)S(4)}, s32[1]{0:T(128)S(4)}) custom-call(s32[3]{0:T(128)} %matchings_hbm.1, bf16[256,128]{1,0:T(8,128)(2,1)} %shape_hbm.1), custom_call_target="tpu_custom_call" | custom-call | tf_op jit(solution)/shard_map/prepare/pallas_call | solution.py:151
  1.5 10.5 %conditional.3 = (f32[8,128]{1,0:T(8,128)S(1)}, bf16[640,128]{1,0:T(8,128)(2,1)S(1)}, bf16[640,256]{1,0:T(8,128)(2,1)S(1)}, bf16[640,256]{1,0:T(8,128)(2,1)S(1)}...) conditional(s32[]{:T(128)} %bitcast, ...), branch_computations={%region_0.0_spmd, %region_1.0_spmd, %region_2.0_spmd, %region_3.0_... | conditional | flops 12589465600 | bytes 129179760 | solution.py:554
  1.6 6.1 %collective-permute-start.13 = (f32[256,128]{1,0:T(8,128)S(1)}, f32[256,128]{1,0:T(8,128)S(1)}, u32[]{:S(2)}, u32[]{:S(2)}) collective-permute-start(f32[256,128]{1,0:T(8,128)S(1)} %get-tuple-element.310), channel_id=1, source_target_pairs={{0,28},{2,30},{4,24},{6,26},{8,20},{10,22},{12,16},{14,18},{16,12}... | collective-permute-start | bytes 393224 | tf_op jit(solution)/shard_map/cond/branch_13_fun/ppermute | solution.py:545
  7.6 2.0 %user_start.28 = (f32[8,128]{1,0:T(8,128)S(1)}, bf16[640,256]{1,0:T(8,128)(2,1)S(1)}, bf16[640,256]{1,0:T(8,128)(2,1)S(1)}, bf16[640,256]{1,0:T(8,128)(2,1)S(1)}...) custom-call(bf16[1280,128]{1,0:T(8,128)(2,1)} %get-tuple-element.302.shape_hbm, ...), custom_call_target="tpu_custom_call" | custom-call | flops 6553600 | bytes 655360 | tf_op jit(solution)/shard_map/cond/branch_13_fun/user_start/pallas_call | solution.py:211
  9.6 1.6 %collective-permute-done.13.refs_2_ = f32[256,128]{1,0:T(8,128)S(1)} collective-permute-done((f32[256,128]{1,0:T(8,128)S(1)}, f32[256,128]{1,0:T(8,128)S(1)}, u32[]{:S(2)}, u32[]{:S(2)}) %collective-permute-start.13) | collective-permute-done | bytes 131104 | tf_op jit(solution)/shard_map/cond/branch_13_fun/ppermute | solution.py:545
  11.2 0.6 stratum0_at0.28
  12.0 1.6 %collective-permute-start.45 = (f32[648,128]{1,0:T(8,128)S(1)}, f32[648,128]{1,0:T(8,128)S(1)}, u32[]{:S(2)}, u32[]{:S(2)}) collective-permute-start(f32[648,128]{1,0:T(8,128)S(1)} %get-tuple-element.477.refs_2_), channel_id=1, source_target_pairs={{0,1},{1,0},{2,3},{3,2},{4,5},{5,4},{6,7},{7,6},{8,9},{9,8},{10,11... | collective-permute-start | bytes 995336 | tf_op jit(solution)/shard_map/ppermute | solution.py:545
  13.6 0.6 %stratum0_at640.1 = (f32[640,128]{1,0:T(8,128)S(1)}, f32[264,128]{1,0:T(8,128)S(1)}) custom-call(bf16[640,256]{1,0:T(8,128)(2,1)S(1)} %get-tuple-element.479.refs_0_, bf16[640,128]{1,0:T(8,128)(2,1)S(1)} %get-tuple-element.480.refs_1_, bf16[256,128]{1,0:T(8,128)(2,1)S(1)} %get-tuple-element.481.refs_2_, f32[256,128]{1,0:T(8,128)S(1)} %get-tuple-element.482.refs_3_, ...), custom_call_target="tpu_custom_call" | custom-call | flops 12582912000 | bytes 128000000 | tf_op jit(solution)/shard_map/stratum0_at640/pallas_call | solution.py:405
  14.2 0.0 copy-start
  14.2 0.6 collective-permute-start.47
  14.8 8.5 %conditional.4 = (bf16[256,128]{1,0:T(8,128)(2,1)S(1)}, f32[264,128]{1,0:T(8,128)S(1)}, f32[8,128]{1,0:T(8,128)S(1)}) conditional(s32[]{:T(128)} %bitcast.1, f32[264,128]{1,0:T(8,128)S(1)} %get-tuple-element.486, f32[264,128]{1,0:T(8,128)S(1)} %get-tuple-element.486, f32[264,128]{1,0:T(8,128)S(1)} %get-tuple-element.486, ...), branch_computations={%region_15.0_spmd, %region_16.0_spmd, %region_17.0_spmd, %region_1... | conditional | flops 1310720 | bytes 868416 | solution.py:554
  14.8 3.4 %collective-permute-start.22 = (f32[264,128]{1,0:T(8,128)S(1)}, f32[264,128]{1,0:T(8,128)S(1)}, u32[]{:S(2)}, u32[]{:S(2)}) collective-permute-start(f32[264,128]{1,0:T(8,128)S(1)} %param.22), channel_id=1, source_target_pairs={{0,16},{2,18},{4,20},{6,22},{8,24},{10,26},{12,28},{14,30},{16,0},... | collective-permute-start | bytes 405512 | tf_op jit(solution)/shard_map/cond/branch_7_fun/ppermute | solution.py:545
  18.2 4.8 %collective-permute-done.22.item = f32[264,128]{1,0:T(8,128)S(1)} collective-permute-done((f32[264,128]{1,0:T(8,128)S(1)}, f32[264,128]{1,0:T(8,128)S(1)}, u32[]{:S(2)}, u32[]{:S(2)}) %collective-permute-start.22) | collective-permute-done | bytes 135200 | tf_op jit(solution)/shard_map/cond/branch_7_fun/ppermute | solution.py:545
  23.0 0.3 meet_items.37
  23.3 0.0 collective-permute-done.45.refs_3_
  23.4 0.0 copy-done
  23.4 1.6 %stratum1_at0.1 = (f32[648,128]{1,0:T(8,128)S(1)}, f32[640,128]{1,0:T(8,128)S(1)}, f32[8,128]{1,0:T(8,128)S(1)}, bf16[640,256]{1,0:T(8,128)(2,1)S(1)}, bf16[640,...) custom-call(bf16[640,256]{1,0:T(8,128)(2,1)S(1)} %get-tuple-element.476, ...), custom_call_target="tpu_custom_call" | custom-call | flops 12582912000 | bytes 128000000 | tf_op jit(solution)/shard_map/stratum1_at0/pallas_call | solution.py:405
  25.0 1.6 %collective-permute-start.46 = (f32[648,128]{1,0:T(8,128)S(1)}, f32[648,128]{1,0:T(8,128)S(1)}, u32[]{:S(2)}, u32[]{:S(2)}) collective-permute-start(f32[648,128]{1,0:T(8,128)S(1)} %get-tuple-element.491.refs_2_), channel_id=1, source_target_pairs={{0,1},{1,0},{2,3},{3,2},{4,5},{5,4},{6,7},{7,6},{8,9},{9,8},{10,11... | collective-permute-start | bytes 995336 | tf_op jit(solution)/shard_map/ppermute | solution.py:545
  26.6 3.3 %collective-permute-done.47.refs_2_ = f32[640,128]{1,0:T(8,128)S(1)} collective-permute-done((f32[640,128]{1,0:T(8,128)S(1)}, f32[640,128]{1,0:T(8,128)S(1)}, u32[]{:S(2)}, u32[]{:S(2)}) %collective-permute-start.47) | collective-permute-done | bytes 327712 | tf_op jit(solution)/shard_map/ppermute | solution.py:545
  29.8 1.0 %stratum1_at640.1 = (f32[640,128]{1,0:T(8,128)S(1)}, f32[640,128]{1,0:T(8,128)S(1)}, f32[264,128]{1,0:T(8,128)S(1)}) custom-call(bf16[640,256]{1,0:T(8,128)(2,1)S(1)} %get-tuple-element.495.refs_0_, f32[640,128]{1,0:T(8,128)S(1)} %get-tuple-element.496.refs_1_, f32[640,128]{1,0:T(8,128)S(1)} %collective-permute-done.47.refs_2_, ...), custom_call_target="tpu_custom_call" | custom-call | flops 12582912000 | bytes 128000000 | tf_op jit(solution)/shard_map/stratum1_at640/pallas_call | solution.py:405
  30.9 1.6 %collective-permute-start.48 = (f32[640,128]{1,0:T(8,128)S(1)}, f32[640,128]{1,0:T(8,128)S(1)}, u32[]{:S(2)}, u32[]{:S(2)}) collective-permute-start(f32[640,128]{1,0:T(8,128)S(1)} %get-tuple-element.505.refs_1_), channel_id=1, source_target_pairs={{0,1},{1,0},{2,3},{3,2},{4,5},{5,4},{6,7},{7,6},{8,9},{9,8},{10,11... | collective-permute-start | bytes 983048 | tf_op jit(solution)/shard_map/ppermute | solution.py:545
  32.4 9.0 %conditional.5 = (bf16[256,128]{1,0:T(8,128)(2,1)S(1)}, f32[264,128]{1,0:T(8,128)S(1)}, f32[8,128]{1,0:T(8,128)S(1)}) conditional(s32[]{:T(128)} %bitcast.2, f32[264,128]{1,0:T(8,128)S(1)} %get-tuple-element.500, f32[264,128]{1,0:T(8,128)S(1)} %get-tuple-element.500, f32[264,128]{1,0:T(8,128)S(1)} %get-tuple-element.500, ...), branch_computations={%region_30.0_spmd, %region_31.0_spmd, %region_32.0_spmd, %region_3... | conditional | flops 1310720 | bytes 868416 | solution.py:554
  32.4 0.0 collective-permute-start.38
  32.4 8.6 %collective-permute-done.38.item = f32[264,128]{1,0:T(8,128)S(1)} collective-permute-done((f32[264,128]{1,0:T(8,128)S(1)}, f32[264,128]{1,0:T(8,128)S(1)}, u32[]{:S(2)}, u32[]{:S(2)}) %collective-permute-start.38) | collective-permute-done | bytes 135200 | tf_op jit(solution)/shard_map/cond/branch_8_fun/ppermute | solution.py:545
  41.1 0.3 meet_items.53
  41.4 0.0 collective-permute-done.46.refs_3_
  41.4 1.5 %stratum2_at0.1 = (f32[648,128]{1,0:T(8,128)S(1)}, f32[640,128]{1,0:T(8,128)S(1)}, f32[8,128]{1,0:T(8,128)S(1)}, bf16[640,256]{1,0:T(8,128)(2,1)S(1)}, bf16[640,...) custom-call(bf16[640,256]{1,0:T(8,128)(2,1)S(1)} %get-tuple-element.490.refs_0_, ...), custom_call_target="tpu_custom_call" | custom-call | flops 12582912000 | bytes 128000000 | tf_op jit(solution)/shard_map/stratum2_at0/pallas_call | solution.py:405
  42.9 0.6 collective-permute-start.53
  43.5 0.0 collective-permute-done.48.refs_2_
  43.6 1.0 %stratum2_at640.1 = (f32[256,128]{1,0:T(8,128)S(1)}, f32[192,128]{1,0:T(8,128)S(1)}, f32[192,128]{1,0:T(8,128)S(1)}, f32[640,128]{1,0:T(8,128)S(1)}, f32[264,128]{1,0:T(8,128)S(1)}) custom-call(bf16[640,256]{1,0:T(8,128)(2,1)S(1)} %get-tuple-element.504.refs_0_, f32[640,128]{1,0:T(8,128)S(1)} %get-tuple-element.505.refs_1_, ...), custom_call_target="tpu_custom_call" | custom-call | flops 12582912000 | bytes 128000000 | tf_op jit(solution)/shard_map/stratum2_at640/pallas_call | solution.py:405
  44.6 2.2 %collective-permute-start.51 = (f32[264,128]{1,0:T(8,128)S(1)}, f32[264,128]{1,0:T(8,128)S(1)}, u32[]{:S(2)}, u32[]{:S(2)}) collective-permute-start(f32[264,128]{1,0:T(8,128)S(1)} %get-tuple-element.514), channel_id=1, source_target_pairs={{0,30},{2,28},{4,26},{6,24},{8,22},{10,20},{12,18},{14,16},{16,14}... | collective-permute-start | bytes 405512 | tf_op jit(solution)/shard_map/ppermute | solution.py:545
  46.8 1.5 %collective-permute-start.52 = (f32[256,128]{1,0:T(8,128)S(1)}, f32[256,128]{1,0:T(8,128)S(1)}, u32[]{:S(2)}, u32[]{:S(2)}) collective-permute-start(f32[256,128]{1,0:T(8,128)S(1)} %get-tuple-element.515.refs_0_), channel_id=1, source_target_pairs={{0,1},{1,0},{2,3},{3,2},{4,5},{5,4},{6,7},{7,6},{8,9},{9,8},{10,11... | collective-permute-start | bytes 393224 | tf_op jit(solution)/shard_map/ppermute | solution.py:545
  48.2 0.5 collective-permute-start.50
  48.8 1.5 %collective-permute-start.49 = (f32[192,128]{1,0:T(8,128)S(1)}, f32[192,128]{1,0:T(8,128)S(1)}, u32[]{:S(2)}, u32[]{:S(2)}) collective-permute-start(f32[192,128]{1,0:T(8,128)S(1)} %get-tuple-element.511.refs_0_), channel_id=1, source_target_pairs={{0,1},{1,0},{2,3},{3,2},{4,5},{5,4},{6,7},{7,6},{8,9},{9,8},{10,11... | collective-permute-start | bytes 294920 | tf_op jit(solution)/shard_map/ppermute | solution.py:545
  50.3 3.4 %collective-permute-done.53.refs_1_ = f32[648,128]{1,0:T(8,128)S(1)} collective-permute-done((f32[648,128]{1,0:T(8,128)S(1)}, f32[648,128]{1,0:T(8,128)S(1)}, u32[]{:S(2)}, u32[]{:S(2)}) %collective-permute-start.53) | collective-permute-done | bytes 331808 | tf_op jit(solution)/shard_map/ppermute | solution.py:545
  53.7 1.3 %user_log_at0.1 = (bf16[1280,128]{1,0:T(8,128)(2,1)}, f32[8,128]{1,0:T(8,128)S(1)}) custom-call(f32[648,128]{1,0:T(8,128)S(1)} %get-tuple-element.516.refs_0_, f32[648,128]{1,0:T(8,128)S(1)} %collective-permute-done.53.refs_1_, f32[640,128]{1,0:T(8,128)S(1)} %get-tuple-element.517.refs_2_, f32[8,128]{1,0:T(8,128)S(1)} %get-tuple-element.507.refs_4_.refs_3_), custom_call_target="tpu_custom_call" | custom-call | flops 3276800 | bytes 1146880 | tf_op jit(solution)/shard_map/user_log_at0/pallas_call | solution.py:501
  55.0 1.5 %collective-permute-done.52.refs_1_ = f32[256,128]{1,0:T(8,128)S(1)} collective-permute-done((f32[256,128]{1,0:T(8,128)S(1)}, f32[256,128]{1,0:T(8,128)S(1)}, u32[]{:S(2)}, u32[]{:S(2)}) %collective-permute-start.52) | collective-permute-done | bytes 131104 | tf_op jit(solution)/shard_map/ppermute | solution.py:545
  56.5 0.9 %user_log_at640.1 = (bf16[1280,128]{1,0:T(8,128)(2,1)}, f32[8,128]{1,0:T(8,128)S(1)}) custom-call(f32[256,128]{1,0:T(8,128)S(1)} %get-tuple-element.515.refs_0_, f32[256,128]{1,0:T(8,128)S(1)} %collective-permute-done.52.refs_1_, f32[640,128]{1,0:T(8,128)S(1)} %get-tuple-element.512.refs_2_, ...), custom_call_target="tpu_custom_call", output_to_operand_aliasing={{0}: (4, {})} | custom-call | flops 1310720 | bytes 458752 | tf_op jit(solution)/shard_map/user_log_at640/pallas_call | solution.py:501
  57.4 0.0 collective-permute-done.51.item
  57.5 0.9 %item_log.1 = (bf16[256,128]{1,0:T(8,128)(2,1)}, f32[8,128]{1,0:T(8,128)S(1)}) custom-call(f32[264,128]{1,0:T(8,128)S(1)} %collective-permute-done.51.item, f32[8,128]{1,0:T(8,128)S(1)} %get-tuple-element.520.through), custom_call_target="tpu_custom_call" | custom-call | flops 1310720 | bytes 196608 | tf_op jit(solution)/shard_map/item_log/pallas_call | solution.py:532
  58.4 0.2 collective-permute-done.50.refs_1_
  58.6 0.9 %user_log_at896.1 = (bf16[1280,128]{1,0:T(8,128)(2,1)}, f32[8,128]{1,0:T(8,128)S(1)}) custom-call(f32[192,128]{1,0:T(8,128)S(1)} %get-tuple-element.513.refs_0_, f32[192,128]{1,0:T(8,128)S(1)} %collective-permute-done.50.refs_1_, f32[640,128]{1,0:T(8,128)S(1)} %get-tuple-element.512.refs_2_, ...), custom_call_target="tpu_custom_call", output_to_operand_aliasing={{0}: (4, {})} | custom-call | flops 983040 | bytes 344064 | tf_op jit(solution)/shard_map/user_log_at896/pallas_call | solution.py:501
  59.5 1.1 %collective-permute-done.49.refs_1_ = f32[192,128]{1,0:T(8,128)S(1)} collective-permute-done((f32[192,128]{1,0:T(8,128)S(1)}, f32[192,128]{1,0:T(8,128)S(1)}, u32[]{:S(2)}, u32[]{:S(2)}) %collective-permute-start.49) | collective-permute-done | bytes 98336 | tf_op jit(solution)/shard_map/ppermute | solution.py:545
  60.6 0.9 %user_log_at1088.1 = bf16[1280,128]{1,0:T(8,128)(2,1)} custom-call(f32[192,128]{1,0:T(8,128)S(1)} %get-tuple-element.511.refs_0_, f32[192,128]{1,0:T(8,128)S(1)} %collective-permute-done.49.refs_1_, f32[640,128]{1,0:T(8,128)S(1)} %get-tuple-element.512.refs_2_, f32[8,128]{1,0:T(8,128)S(1)} %get-tuple-element.523.refs_3_, ...), custom_call_target="tpu_custom_call", output_to_operand_aliasing={{}: (4, {})} | custom-call | flops 983040 | bytes 344064 | tf_op jit(solution)/shard_map/user_log_at1088/pallas_call | solution.py:501
Async XLA Ops:
  1.6 9.7 %collective-permute-start.13 = (f32[256,128]{1,0:T(8,128)S(1)}, f32[256,128]{1,0:T(8,128)S(1)}, u32[]{:S(2)}, u32[]{:S(2)}) collective-permute-start(f32[256,128]{1,0:T(8,128)S(1)} %get-tuple-element.310), channel_id=1, source_target_pairs={{0,28},{2,30},{4,24},{6,26},{8,20},{10,22},{12,16},{14,18},{16,12}... | collective-permute-start | bytes 393224 | tf_op jit(solution)/shard_map/cond/branch_13_fun/ppermute | solution.py:545
  12.0 11.3 %collective-permute-start.45 = (f32[648,128]{1,0:T(8,128)S(1)}, f32[648,128]{1,0:T(8,128)S(1)}, u32[]{:S(2)}, u32[]{:S(2)}) collective-permute-start(f32[648,128]{1,0:T(8,128)S(1)} %get-tuple-element.477.refs_2_), channel_id=1, source_target_pairs={{0,1},{1,0},{2,3},{3,2},{4,5},{5,4},{6,7},{7,6},{8,9},{9,8},{10,11... | collective-permute-start | bytes 995336 | tf_op jit(solution)/shard_map/ppermute | solution.py:545
  14.2 9.1 %copy-start = (bf16[1280,128]{1,0:T(8,128)(2,1)S(1)}, bf16[1280,128]{1,0:T(8,128)(2,1)}, u32[]{:S(2)}) copy-start(bf16[1280,128]{1,0:T(8,128)(2,1)} %refs_3_.1) | copy-start | bytes 983044
  14.2 15.6 %collective-permute-start.47 = (f32[640,128]{1,0:T(8,128)S(1)}, f32[640,128]{1,0:T(8,128)S(1)}, u32[]{:S(2)}, u32[]{:S(2)}) collective-permute-start(f32[640,128]{1,0:T(8,128)S(1)} %get-tuple-element.496.refs_1_), channel_id=1, source_target_pairs={{0,1},{1,0},{2,3},{3,2},{4,5},{5,4},{6,7},{7,6},{8,9},{9,8},{10,11... | collective-permute-start | bytes 983048 | tf_op jit(solution)/shard_map/ppermute | solution.py:545
  14.8 8.2 %collective-permute-start.22 = (f32[264,128]{1,0:T(8,128)S(1)}, f32[264,128]{1,0:T(8,128)S(1)}, u32[]{:S(2)}, u32[]{:S(2)}) collective-permute-start(f32[264,128]{1,0:T(8,128)S(1)} %param.22), channel_id=1, source_target_pairs={{0,16},{2,18},{4,20},{6,22},{8,24},{10,26},{12,28},{14,30},{16,0},... | collective-permute-start | bytes 405512 | tf_op jit(solution)/shard_map/cond/branch_7_fun/ppermute | solution.py:545
  25.0 16.4 %collective-permute-start.46 = (f32[648,128]{1,0:T(8,128)S(1)}, f32[648,128]{1,0:T(8,128)S(1)}, u32[]{:S(2)}, u32[]{:S(2)}) collective-permute-start(f32[648,128]{1,0:T(8,128)S(1)} %get-tuple-element.491.refs_2_), channel_id=1, source_target_pairs={{0,1},{1,0},{2,3},{3,2},{4,5},{5,4},{6,7},{7,6},{8,9},{9,8},{10,11... | collective-permute-start | bytes 995336 | tf_op jit(solution)/shard_map/ppermute | solution.py:545
  30.9 12.7 %collective-permute-start.48 = (f32[640,128]{1,0:T(8,128)S(1)}, f32[640,128]{1,0:T(8,128)S(1)}, u32[]{:S(2)}, u32[]{:S(2)}) collective-permute-start(f32[640,128]{1,0:T(8,128)S(1)} %get-tuple-element.505.refs_1_), channel_id=1, source_target_pairs={{0,1},{1,0},{2,3},{3,2},{4,5},{5,4},{6,7},{7,6},{8,9},{9,8},{10,11... | collective-permute-start | bytes 983048 | tf_op jit(solution)/shard_map/ppermute | solution.py:545
  32.4 8.6 %collective-permute-start.38 = (f32[264,128]{1,0:T(8,128)S(1)}, f32[264,128]{1,0:T(8,128)S(1)}, u32[]{:S(2)}, u32[]{:S(2)}) collective-permute-start(f32[264,128]{1,0:T(8,128)S(1)} %param.38), channel_id=1, source_target_pairs={{0,18},{2,16},{4,22},{6,20},{8,26},{10,24},{12,30},{14,28},{16,2},... | collective-permute-start | bytes 405512 | tf_op jit(solution)/shard_map/cond/branch_8_fun/ppermute | solution.py:545
  42.9 10.7 %collective-permute-start.53 = (f32[648,128]{1,0:T(8,128)S(1)}, f32[648,128]{1,0:T(8,128)S(1)}, u32[]{:S(2)}, u32[]{:S(2)}) collective-permute-start(f32[648,128]{1,0:T(8,128)S(1)} %get-tuple-element.516.refs_0_), channel_id=1, source_target_pairs={{0,1},{1,0},{2,3},{3,2},{4,5},{5,4},{6,7},{7,6},{8,9},{9,8},{10,11... | collective-permute-start | bytes 995336 | tf_op jit(solution)/shard_map/ppermute | solution.py:545
  44.6 12.9 %collective-permute-start.51 = (f32[264,128]{1,0:T(8,128)S(1)}, f32[264,128]{1,0:T(8,128)S(1)}, u32[]{:S(2)}, u32[]{:S(2)}) collective-permute-start(f32[264,128]{1,0:T(8,128)S(1)} %get-tuple-element.514), channel_id=1, source_target_pairs={{0,30},{2,28},{4,26},{6,24},{8,22},{10,20},{12,18},{14,16},{16,14}... | collective-permute-start | bytes 405512 | tf_op jit(solution)/shard_map/ppermute | solution.py:545
  46.8 9.7 %collective-permute-start.52 = (f32[256,128]{1,0:T(8,128)S(1)}, f32[256,128]{1,0:T(8,128)S(1)}, u32[]{:S(2)}, u32[]{:S(2)}) collective-permute-start(f32[256,128]{1,0:T(8,128)S(1)} %get-tuple-element.515.refs_0_), channel_id=1, source_target_pairs={{0,1},{1,0},{2,3},{3,2},{4,5},{5,4},{6,7},{7,6},{8,9},{9,8},{10,11... | collective-permute-start | bytes 393224 | tf_op jit(solution)/shard_map/ppermute | solution.py:545
  48.2 10.4 %collective-permute-start.50 = (f32[192,128]{1,0:T(8,128)S(1)}, f32[192,128]{1,0:T(8,128)S(1)}, u32[]{:S(2)}, u32[]{:S(2)}) collective-permute-start(f32[192,128]{1,0:T(8,128)S(1)} %get-tuple-element.513.refs_0_), channel_id=1, source_target_pairs={{0,1},{1,0},{2,3},{3,2},{4,5},{5,4},{6,7},{7,6},{8,9},{9,8},{10,11... | collective-permute-start | bytes 294920 | tf_op jit(solution)/shard_map/ppermute | solution.py:545
  48.8 11.8 %collective-permute-start.49 = (f32[192,128]{1,0:T(8,128)S(1)}, f32[192,128]{1,0:T(8,128)S(1)}, u32[]{:S(2)}, u32[]{:S(2)}) collective-permute-start(f32[192,128]{1,0:T(8,128)S(1)} %get-tuple-element.511.refs_0_), channel_id=1, source_target_pairs={{0,1},{1,0},{2,3},{3,2},{4,5},{5,4},{6,7},{7,6},{8,9},{9,8},{10,11... | collective-permute-start | bytes 294920 | tf_op jit(solution)/shard_map/ppermute | solution.py:545

commit v4 on v2

--- a/solution.py
+++ b/solution.py
@@ -224,6 +224,32 @@
     return theta, arrays[:len(ahead)], arrays[len(ahead):]
 
 
+def fetch_kernel(interactions, *refs, ahead):
+    counts, sems = refs[:-1], refs[-1]
+    fetches = [
+        pltpu.make_async_copy(interactions.at[s, pl.ds(at, rows), :], counts[i], sems.at[i])
+        for i, (s, at, rows) in enumerate(ahead)]
+    for fetch in fetches:
+        fetch.start()
+    for fetch in fetches:
+        fetch.wait()
+
+
+def fetch_call(interactions, ahead):
+    items = interactions.shape[2]
+    return pl.pallas_call(
+        functools.partial(fetch_kernel, ahead=ahead),
+        out_shape=[pltpu.VMEM((rows, items), BF16) for _, _, rows in ahead],
+        in_specs=[HBM_SPEC],
+        out_specs=[VMEM_SPEC] * len(ahead),
+        scratch_shapes=[pltpu.SemaphoreType.DMA((len(ahead),))],
+        compiler_params=PARAMS,
+        cost_estimate=pl.CostEstimate(
+            flops=0, bytes_accessed=4 * items * sum(rows for _, _, rows in ahead), transcendentals=0),
+        name="fetch_weights",
+    )(in_hbm(interactions))
+
+
 def dot_rows(a, b):
     return lax.dot_general(a, b, (((1,), (1,)), ((), ())), preferred_element_type=F32)
 
@@ -232,7 +258,7 @@
     return lax.dot_general(ratios[...], uexp[...], (((0,), (0,)), ((), ())), preferred_element_type=F32)
 
 
-def stratum_kernel(names, *refs, stratum, at, rows, items, factor, first, last, earlier, cuts, ahead):
+def stratum_kernel(names, *refs, stratum, at, rows, items, factor, first, last, earlier, cuts):
     ref = dict(zip(names, refs))
     copies = {}
 
@@ -242,8 +268,6 @@
 
     if first and stratum > 0:
         fetch("item", ref["item"], ref["item_kept"])
-    for i, (s, begin, size) in enumerate(ahead):
-        fetch(f"ahead{i}", ref["interactions"].at[s, pl.ds(begin, size), :], ref[f"counts_ahead{i}"])
     upart, counts, ratios, denominator = ref["upart0"], ref["counts"], ref["ratios"], ref["denominator"]
     uexp = ref["uexp"]
     extra = 8 if first else 0
@@ -364,11 +388,8 @@
                     redo_loop(rows if pair[0] is ratios else pair[0].shape[0], redo_stat)
                 update_items(total[...])
 
-    for i in range(len(ahead)):
-        copies[f"ahead{i}"].wait()
-
-
-def stratum_call(stratum, at, rows, items, depth, factor, first, last, earlier, cuts, ahead, operands):
+
+def stratum_call(stratum, at, rows, items, depth, factor, first, last, earlier, cuts, operands):
     extra = 8 if first else 0
     outs = {f"upart{i}": ((size + (0 if i else extra), depth), F32) for i, size in enumerate(cuts)}
     if stratum > 0:
@@ -386,25 +407,23 @@
         outs["uexp"] = ((rows, depth), BF16)
         if stratum > 0:
             outs["theta_new"] = ((8, depth), F32)
-    for i, fetch in enumerate(ahead):
-        outs[f"counts_ahead{i}"] = ((fetch[2], items), BF16)
     scratch = {
         "denominator": pltpu.VMEM((rows, items), F32),
-        "sems": pltpu.SemaphoreType.DMA((1 + len(ahead),)),
+        "sems": pltpu.SemaphoreType.DMA((1,)),
     }
     if last:
         scratch["ratios"] = pltpu.VMEM((rows, items), BF16)
         if stratum > 0:
             scratch["uexp"] = pltpu.VMEM((rows, depth), BF16)
             scratch["theta_new"] = pltpu.VMEM((8, depth), F32)
-    hbm = ("interactions", "item") if stratum > 0 else ("interactions",)
+    hbm = ("item",) if stratum > 0 else ()
     operands = {
         name: in_hbm(x) if name in hbm else in_vmem(x) if name in ("user_shape", "item") else x
         for name, x in operands.items()}
     names = list(operands) + list(outs) + list(scratch)
     kernel = functools.partial(
         stratum_kernel, names, stratum=stratum, at=at, rows=rows, items=items,
-        factor=factor, first=first, last=last, earlier=earlier, cuts=cuts, ahead=ahead)
+        factor=factor, first=first, last=last, earlier=earlier, cuts=cuts)
     results = pl.pallas_call(
         kernel,
         out_shape=[jax.ShapeDtypeStruct(*spec) for spec in outs.values()],
@@ -541,17 +560,16 @@
     item, choices = prepare_call(matchings, item_shape, group - 1)
     order = [(s, at, rows) for s in range(STRATA) for at, rows in zip(starts, sizes)]
 
-    def ahead_of(stratum):
-        begin = 0 if stratum == 0 else stratum * count + 1
-        return order[begin:(stratum + 1) * count + 1]
+    def chunks_of(stratum):
+        return order[stratum * count:(stratum + 1) * count]
 
     def opening(arrived, user_shape, interactions):
-        theta, counts, uexps = start_call(user_shape, interactions, sizes, ahead_of(0))
+        theta, counts, uexps = start_call(user_shape, interactions, sizes, chunks_of(0))
         operands = {"counts": counts[0], "uexp_in": uexps[0], "item": arrived}
         if count == 1:
             operands["theta"] = theta
         out = stratum_call(
-            0, 0, sizes[0], items, depth, factor, True, count == 1, 0, sizes[:1], [], operands)
+            0, 0, sizes[0], items, depth, factor, True, count == 1, 0, sizes[:1], operands)
         return theta, [out["uexp"], *uexps[1:]], counts[1:], out
 
     theta, uexps, fetched, opened = moved(choices[0], item, opening, (user_shape, interactions))
@@ -564,13 +582,10 @@
         for i, (at, rows) in enumerate(zip(starts, sizes)):
             first, last = i == 0, i == count - 1
             step = stratum * count + i
-            ahead = ahead_of(stratum) if first and stratum > 0 else []
             cuts = last_cuts(rows) if step + 1 == len(order) else [rows]
             operands = {}
             if step:
                 operands["counts"], fetched = fetched[0], fetched[1:]
-            if ahead:
-                operands["interactions"] = interactions
             if stratum == 0:
                 operands["uexp"] = uexps[i]
             else:
@@ -597,8 +612,7 @@
                 out = opened
             else:
                 out = stratum_call(
-                    stratum, at, rows, items, depth, factor, first, last, i, cuts, ahead, operands)
-            fetched = [*fetched, *(out[f"counts_ahead{n}"] for n in range(len(ahead)))]
+                    stratum, at, rows, items, depth, factor, first, last, i, cuts, operands)
             shp[i] = out.get("shp_new")
             sums[i] = exchanged(out["upart0"])
             if first:
@@ -612,7 +626,10 @@
                 if stratum > 0:
                     carried["theta"] = out["theta_new"]
         if stratum + 1 < STRATA:
-            item = moved(choices[stratum + 1], item)
+            def with_weights(arrived, interactions, chunks=chunks_of(stratum + 1)):
+                return arrived, fetch_call(interactions, chunks)
+
+            item, fetched = moved(choices[stratum + 1], item, with_weights, (interactions,))
         else:
             item = swapped(item, "users", group - 1)
     user_log = None

time: 59.4 us -> 61.1 us (1.029); the launches traced: 59.6 us -> 60.2 us
  waiting for transfers between devices: 25 us -> 19.9 us
  starting transfers between devices: 19.4 us -> 22.9 us
  Pallas kernels: 14.1 us -> 16.2 us
    ppermute x12, waiting for transfers between devices: 25 us -> 19.9 us  [swapped(): lax.ppermute(value, axis, [(a, a ^ mask) for a in range(lax.axis_size(axi...]
    ppermute x12, starting transfers between devices: 19.4 us -> 22.9 us  [swapped(): lax.ppermute(value, axis, [(a, a ^ mask) for a in range(lax.axis_size(axi...]
    pallas_call x0 -> x2, Pallas kernels: none -> 2.17 us  [fetch_call(): pl.pallas_call(functools.partial(fetch_kernel, ahead=ahead), out_shape=[p...]
  transfers between devices with their start and end apart: 12 -> 12, of which waited for: 9 -> 8; matrix products, arithmetic and copies ran while one was open for 0% -> 0% of each run, Pallas kernels for 20% -> 23%
where the time goes in v4:
time: 61.1 us; the launch traced here: 60.2 us
  starting transfers between devices  22.9 us (37%)
  waiting for transfers between devices  19.9 us (33%)
  Pallas kernels  16.2 us (27%)
  between operations  0.91 us (1%)
    ppermute x12, starting transfers between devices, swapped(): lax.ppermute(value, axis, [(a, a ^ mask) for a in range(lax.axis_size(axi...  22.9 us
    ppermute x12, waiting for transfers between devices, swapped(): lax.ppermute(value, axis, [(a, a ^ mask) for a in range(lax.axis_size(axi...  19.9 us
    pallas_call x6, Pallas kernels, stratum_call(): pl.pallas_call(kernel, out_shape=[jax.ShapeDtypeStruct(*spec) for spec in...  6.28 us
    pallas_call x4, Pallas kernels, user_log_call(): pl.pallas_call(functools.partial(user_log_kernel, at=at, rows=rows, shp_a...  3.96 us
    pallas_call x2, Pallas kernels, fetch_call(): pl.pallas_call(functools.partial(fetch_kernel, ahead=ahead), out_shape=[p...  2.17 us
    pallas_call x1, Pallas kernels, start_call(): pl.pallas_call(functools.partial(start_kernel, ahead=ahead), out_shape=[p...  1.97 us
  transfers between devices with their start and end apart: 12, of which 8 were waited for; matrix products, arithmetic and copies ran while one was open for 0% of the time, Pallas kernels for 23%

profile of v4, /device:TPU:0, one launch (start us, length us, event | category | flops | bytes accessed | tf_op | source)
XLA Modules:
  0.0 60.2 jit_solution(9939064017824886153)
XLA Ops:
  0.6 0.9 %prepare.1 = (f32[256,128]{1,0:T(8,128)S(1)}, s32[1]{0:T(128)S(4)}, s32[1]{0:T(128)S(4)}, s32[1]{0:T(128)S(4)}) custom-call(s32[3]{0:T(128)} %matchings_hbm.1, bf16[256,128]{1,0:T(8,128)(2,1)} %shape_hbm.1), custom_call_target="tpu_custom_call" | custom-call | tf_op jit(solution)/shard_map/prepare/pallas_call | solution.py:151
  1.5 11.4 %conditional.3 = (f32[8,128]{1,0:T(8,128)S(1)}, bf16[640,128]{1,0:T(8,128)(2,1)S(1)}, bf16[640,256]{1,0:T(8,128)(2,1)S(1)}, bf16[256,128]{1,0:T(8,128)(2,1)S(1)}...) conditional(s32[]{:T(128)} %bitcast.2, ...), branch_computations={%region_0.0_spmd, %region_1.0_spmd, %region_2.0_spmd, %region_3.0_... | conditional | flops 12589465600 | bytes 129179752 | solution.py:537
  1.6 4.5 %collective-permute-start.10 = (f32[256,128]{1,0:T(8,128)S(1)}, f32[256,128]{1,0:T(8,128)S(1)}, u32[]{:S(2)}, u32[]{:S(2)}) collective-permute-start(f32[256,128]{1,0:T(8,128)S(1)} %get-tuple-element.347), channel_id=1, source_target_pairs={{0,22},{2,20},{4,18},{6,16},{8,30},{10,28},{12,26},{14,24},{16,6},... | collective-permute-start | bytes 393224 | tf_op jit(solution)/shard_map/cond/branch_10_fun/ppermute | solution.py:528
  6.1 2.0 %user_start.25 = (f32[8,128]{1,0:T(8,128)S(1)}, bf16[640,256]{1,0:T(8,128)(2,1)S(1)}, bf16[640,256]{1,0:T(8,128)(2,1)S(1)}, bf16[640,128]{1,0:T(8,128)(2,1)S(1)}, bf16[640,128]{1,0:T(8,128)(2,1)S(1)}) custom-call(bf16[1280,128]{1,0:T(8,128)(2,1)} %get-tuple-element.340.shape_hbm, bf16[3,1280,256]{2,1,0:T(8,128)(2,1)} %get-tuple-element.341.interactions), custom_call_target="tpu_custom_call" | custom-call | flops 6553600 | bytes 655360 | tf_op jit(solution)/shard_map/cond/branch_10_fun/user_start/pallas_call | solution.py:211
  8.0 4.1 %collective-permute-done.10.refs_2_ = f32[256,128]{1,0:T(8,128)S(1)} collective-permute-done((f32[256,128]{1,0:T(8,128)S(1)}, f32[256,128]{1,0:T(8,128)S(1)}, u32[]{:S(2)}, u32[]{:S(2)}) %collective-permute-start.10) | collective-permute-done | bytes 131104 | tf_op jit(solution)/shard_map/cond/branch_10_fun/ppermute | solution.py:528
  12.1 0.6 stratum0_at0.25
  12.9 2.6 %collective-permute-start.46 = (f32[648,128]{1,0:T(8,128)S(1)}, f32[648,128]{1,0:T(8,128)S(1)}, u32[]{:S(2)}, u32[]{:S(2)}) collective-permute-start(f32[648,128]{1,0:T(8,128)S(1)} %get-tuple-element.594.refs_1_), channel_id=1, source_target_pairs={{0,1},{1,0},{2,3},{3,2},{4,5},{5,4},{6,7},{7,6},{8,9},{9,8},{10,11... | collective-permute-start | bytes 995336 | tf_op jit(solution)/shard_map/ppermute | solution.py:528
  15.5 0.6 %stratum0_at640.1 = (f32[640,128]{1,0:T(8,128)S(1)}, f32[264,128]{1,0:T(8,128)S(1)}) custom-call(bf16[640,256]{1,0:T(8,128)(2,1)S(1)} %get-tuple-element.583.refs_0_, bf16[640,128]{1,0:T(8,128)(2,1)S(1)} %get-tuple-element.584.refs_1_, f32[256,128]{1,0:T(8,128)S(1)} %get-tuple-element.585.refs_2_, bf16[256,128]{1,0:T(8,128)(2,1)S(1)} %get-tuple-element.586.refs_3_, ...), custom_call_target="tpu_custom_call" | custom-call | flops 12582912000 | bytes 128000000 | tf_op jit(solution)/shard_map/stratum0_at640/pallas_call | solution.py:427
  16.2 0.1 collective-permute-start.45
  16.3 0.0 copy-start
  16.3 9.3 %conditional.4 = (f32[264,128]{1,0:T(8,128)}, bf16[640,256]{1,0:T(8,128)(2,1)S(1)}, bf16[640,256]{1,0:T(8,128)(2,1)S(1)}) conditional(s32[]{:T(128)} %bitcast.1, (f32[264,128]{1,0:T(8,128)S(1)}, bf16[3,1280,256]{2,1,0:T(8,128)(2,1)}) %tuple.189, (f32[264,128]{1,0:T(8,128)S(1)}, ...), branch_computations={%region_15.0_spmd, %region_16.0_spmd, %region_17.0_spmd, %region_1... | conditional | bytes 1851456 | solution.py:537
  16.3 0.6 %collective-permute-start.22 = (f32[264,128]{1,0:T(8,128)S(1)}, f32[264,128]{1,0:T(8,128)}, u32[]{:S(2)}, u32[]{:S(2)}) collective-permute-start(f32[264,128]{1,0:T(8,128)S(1)} %get-tuple-element.433), channel_id=1, source_target_pairs={{0,16},{2,18},{4,20},{6,22},{8,24},{10,26},{12,28},{14,30},{16,0},... | collective-permute-start | bytes 405512 | tf_op jit(solution)/shard_map/cond/branch_7_fun/ppermute | solution.py:528
  16.9 1.1 %fetch_weights.37 = (bf16[640,256]{1,0:T(8,128)(2,1)S(1)}, bf16[640,256]{1,0:T(8,128)(2,1)S(1)}) custom-call(bf16[3,1280,256]{2,1,0:T(8,128)(2,1)} %get-tuple-element.434.interactions), custom_call_target="tpu_custom_call" | custom-call | bytes 1310720 | tf_op jit(solution)/shard_map/cond/branch_7_fun/fetch_weights/pallas_call | solution.py:240
  18.0 7.6 %collective-permute-done.22 = f32[264,128]{1,0:T(8,128)} collective-permute-done((f32[264,128]{1,0:T(8,128)S(1)}, f32[264,128]{1,0:T(8,128)}, u32[]{:S(2)}, u32[]{:S(2)}) %collective-permute-start.22) | collective-permute-done | bytes 135200 | tf_op jit(solution)/shard_map/cond/branch_7_fun/ppermute | solution.py:528
  25.6 0.0 collective-permute-done.46.refs_2_
  25.6 0.0 copy-done
  25.6 1.5 %stratum1_at0.1 = (f32[648,128]{1,0:T(8,128)S(1)}, f32[640,128]{1,0:T(8,128)S(1)}, f32[8,128]{1,0:T(8,128)S(1)}, bf16[256,128]{1,0:T(8,128)(2,1)S(1)}, f32[264,1...) custom-call(bf16[640,256]{1,0:T(8,128)(2,1)S(1)} %get-tuple-element.593.refs_, ...), custom_call_target="tpu_custom_call" | custom-call | flops 12582912000 | bytes 128000000 | tf_op jit(solution)/shard_map/stratum1_at0/pallas_call | solution.py:427
  27.1 1.7 %collective-permute-start.48 = (f32[648,128]{1,0:T(8,128)S(1)}, f32[648,128]{1,0:T(8,128)S(1)}, u32[]{:S(2)}, u32[]{:S(2)}) collective-permute-start(f32[648,128]{1,0:T(8,128)S(1)} %get-tuple-element.607.refs_1_), channel_id=1, source_target_pairs={{0,1},{1,0},{2,3},{3,2},{4,5},{5,4},{6,7},{7,6},{8,9},{9,8},{10,11... | collective-permute-start | bytes 995336 | tf_op jit(solution)/shard_map/ppermute | solution.py:528
  28.8 2.3 %collective-permute-done.45.refs_2_ = f32[640,128]{1,0:T(8,128)S(1)} collective-permute-done((f32[640,128]{1,0:T(8,128)S(1)}, f32[640,128]{1,0:T(8,128)S(1)}, u32[]{:S(2)}, u32[]{:S(2)}) %collective-permute-start.45) | collective-permute-done | bytes 327712 | tf_op jit(solution)/shard_map/ppermute | solution.py:528
  31.1 1.0 %stratum1_at640.1 = (f32[640,128]{1,0:T(8,128)S(1)}, f32[640,128]{1,0:T(8,128)S(1)}, f32[264,128]{1,0:T(8,128)S(1)}) custom-call(bf16[640,256]{1,0:T(8,128)(2,1)S(1)} %get-tuple-element.591.refs_0_, f32[640,128]{1,0:T(8,128)S(1)} %get-tuple-element.592.refs_1_, f32[640,128]{1,0:T(8,128)S(1)} %collective-permute-done.45.refs_2_, ...), custom_call_target="tpu_custom_call" | custom-call | flops 12582912000 | bytes 128000000 | tf_op jit(solution)/shard_map/stratum1_at640/pallas_call | solution.py:427
  32.2 2.1 %collective-permute-start.47 = (f32[640,128]{1,0:T(8,128)S(1)}, f32[640,128]{1,0:T(8,128)S(1)}, u32[]{:S(2)}, u32[]{:S(2)}) collective-permute-start(f32[640,128]{1,0:T(8,128)S(1)} %get-tuple-element.604.refs_1_), channel_id=1, source_target_pairs={{0,1},{1,0},{2,3},{3,2},{4,5},{5,4},{6,7},{7,6},{8,9},{9,8},{10,11... | collective-permute-start | bytes 983048 | tf_op jit(solution)/shard_map/ppermute | solution.py:528
  34.3 7.0 %conditional.5 = (f32[264,128]{1,0:T(8,128)}, bf16[640,256]{1,0:T(8,128)(2,1)S(1)}, bf16[640,256]{1,0:T(8,128)(2,1)S(1)}) conditional(s32[]{:T(128)} %bitcast, (f32[264,128]{1,0:T(8,128)S(1)}, bf16[3,1280,256]{2,1,0:T(8,128)(2,1)}) %tuple.190, (f32[264,128]{1,0:T(8,128)S(1)}, ...), branch_computations={%region_30.0_spmd, %region_31.0_spmd, %region_32.0_spmd, %region_3... | conditional | bytes 1851456 | solution.py:537
  34.3 3.8 %collective-permute-start.41 = (f32[264,128]{1,0:T(8,128)S(1)}, f32[264,128]{1,0:T(8,128)}, u32[]{:S(2)}, u32[]{:S(2)}) collective-permute-start(f32[264,128]{1,0:T(8,128)S(1)} %get-tuple-element.509), channel_id=1, source_target_pairs={{0,24},{2,26},{4,28},{6,30},{8,16},{10,18},{12,20},{14,22},{16,8},... | collective-permute-start | bytes 405512 | tf_op jit(solution)/shard_map/cond/branch_11_fun/ppermute | solution.py:528
  38.1 1.1 %fetch_weights.56 = (bf16[640,256]{1,0:T(8,128)(2,1)S(1)}, bf16[640,256]{1,0:T(8,128)(2,1)S(1)}) custom-call(bf16[3,1280,256]{2,1,0:T(8,128)(2,1)} %get-tuple-element.510.interactions), custom_call_target="tpu_custom_call" | custom-call | bytes 1310720 | tf_op jit(solution)/shard_map/cond/branch_11_fun/fetch_weights/pallas_call | solution.py:240
  39.2 2.1 %collective-permute-done.41 = f32[264,128]{1,0:T(8,128)} collective-permute-done((f32[264,128]{1,0:T(8,128)S(1)}, f32[264,128]{1,0:T(8,128)}, u32[]{:S(2)}, u32[]{:S(2)}) %collective-permute-start.41) | collective-permute-done | bytes 135200 | tf_op jit(solution)/shard_map/cond/branch_11_fun/ppermute | solution.py:528
  41.3 0.0 collective-permute-done.48.refs_2_
  41.3 1.5 %stratum2_at0.1 = (f32[648,128]{1,0:T(8,128)S(1)}, f32[640,128]{1,0:T(8,128)S(1)}, f32[8,128]{1,0:T(8,128)S(1)}, bf16[256,128]{1,0:T(8,128)(2,1)S(1)}, f32[264,1...) custom-call(bf16[640,256]{1,0:T(8,128)(2,1)S(1)} %get-tuple-element.606.refs_, ...), custom_call_target="tpu_custom_call" | custom-call | flops 12582912000 | bytes 128000000 | tf_op jit(solution)/shard_map/stratum2_at0/pallas_call | solution.py:427
  42.8 0.6 collective-permute-start.53
  43.4 1.9 %collective-permute-done.47.refs_2_ = f32[640,128]{1,0:T(8,128)S(1)} collective-permute-done((f32[640,128]{1,0:T(8,128)S(1)}, f32[640,128]{1,0:T(8,128)S(1)}, u32[]{:S(2)}, u32[]{:S(2)}) %collective-permute-start.47) | collective-permute-done | bytes 327712 | tf_op jit(solution)/shard_map/ppermute | solution.py:528
  45.3 1.0 %stratum2_at640.1 = (f32[256,128]{1,0:T(8,128)S(1)}, f32[192,128]{1,0:T(8,128)S(1)}, f32[192,128]{1,0:T(8,128)S(1)}, f32[640,128]{1,0:T(8,128)S(1)}, f32[264,128]{1,0:T(8,128)S(1)}) custom-call(bf16[640,256]{1,0:T(8,128)(2,1)S(1)} %get-tuple-element.603.refs_0_, f32[640,128]{1,0:T(8,128)S(1)} %get-tuple-element.604.refs_1_, ...), custom_call_target="tpu_custom_call" | custom-call | flops 12582912000 | bytes 128000000 | tf_op jit(solution)/shard_map/stratum2_at640/pallas_call | solution.py:427
  46.3 3.4 %collective-permute-start.51 = (f32[264,128]{1,0:T(8,128)S(1)}, f32[264,128]{1,0:T(8,128)S(1)}, u32[]{:S(2)}, u32[]{:S(2)}) collective-permute-start(f32[264,128]{1,0:T(8,128)S(1)} %get-tuple-element.619), channel_id=1, source_target_pairs={{0,30},{2,28},{4,26},{6,24},{8,22},{10,20},{12,18},{14,16},{16,14}... | collective-permute-start | bytes 405512 | tf_op jit(solution)/shard_map/ppermute | solution.py:528
  49.7 1.5 %collective-permute-start.52 = (f32[256,128]{1,0:T(8,128)S(1)}, f32[256,128]{1,0:T(8,128)S(1)}, u32[]{:S(2)}, u32[]{:S(2)}) collective-permute-start(f32[256,128]{1,0:T(8,128)S(1)} %get-tuple-element.620.refs_0_), channel_id=1, source_target_pairs={{0,1},{1,0},{2,3},{3,2},{4,5},{5,4},{6,7},{7,6},{8,9},{9,8},{10,11... | collective-permute-start | bytes 393224 | tf_op jit(solution)/shard_map/ppermute | solution.py:528
  51.2 0.5 collective-permute-start.50
  51.8 1.5 %collective-permute-start.49 = (f32[192,128]{1,0:T(8,128)S(1)}, f32[192,128]{1,0:T(8,128)S(1)}, u32[]{:S(2)}, u32[]{:S(2)}) collective-permute-start(f32[192,128]{1,0:T(8,128)S(1)} %get-tuple-element.616.refs_0_), channel_id=1, source_target_pairs={{0,1},{1,0},{2,3},{3,2},{4,5},{5,4},{6,7},{7,6},{8,9},{9,8},{10,11... | collective-permute-start | bytes 294920 | tf_op jit(solution)/shard_map/ppermute | solution.py:528
  53.2 0.0 collective-permute-done.53.refs_1_
  53.2 1.3 %user_log_at0.1 = (bf16[1280,128]{1,0:T(8,128)(2,1)}, f32[8,128]{1,0:T(8,128)S(1)}) custom-call(f32[648,128]{1,0:T(8,128)S(1)} %get-tuple-element.621.refs_0_, f32[648,128]{1,0:T(8,128)S(1)} %collective-permute-done.53.refs_1_, f32[640,128]{1,0:T(8,128)S(1)} %get-tuple-element.622.refs_2_, f32[8,128]{1,0:T(8,128)S(1)} %get-tuple-element.610.refs_4_.refs_3_), custom_call_target="tpu_custom_call" | custom-call | flops 3276800 | bytes 1146880 | tf_op jit(solution)/shard_map/user_log_at0/pallas_call | solution.py:484
  54.5 0.5 collective-permute-done.52.refs_1_
  55.0 0.9 %user_log_at640.1 = (bf16[1280,128]{1,0:T(8,128)(2,1)}, f32[8,128]{1,0:T(8,128)S(1)}) custom-call(f32[256,128]{1,0:T(8,128)S(1)} %get-tuple-element.620.refs_0_, f32[256,128]{1,0:T(8,128)S(1)} %collective-permute-done.52.refs_1_, f32[640,128]{1,0:T(8,128)S(1)} %get-tuple-element.617.refs_2_, ...), custom_call_target="tpu_custom_call", output_to_operand_aliasing={{0}: (4, {})} | custom-call | flops 1310720 | bytes 458752 | tf_op jit(solution)/shard_map/user_log_at640/pallas_call | solution.py:484
  55.9 0.0 collective-permute-done.51.item
  55.9 0.9 %item_log.1 = (bf16[256,128]{1,0:T(8,128)(2,1)}, f32[8,128]{1,0:T(8,128)S(1)}) custom-call(f32[264,128]{1,0:T(8,128)S(1)} %collective-permute-done.51.item, f32[8,128]{1,0:T(8,128)S(1)} %get-tuple-element.625.through), custom_call_target="tpu_custom_call" | custom-call | flops 1310720 | bytes 196608 | tf_op jit(solution)/shard_map/item_log/pallas_call | solution.py:515
  56.9 0.2 collective-permute-done.50.refs_1_
  57.1 0.9 %user_log_at896.1 = (bf16[1280,128]{1,0:T(8,128)(2,1)}, f32[8,128]{1,0:T(8,128)S(1)}) custom-call(f32[192,128]{1,0:T(8,128)S(1)} %get-tuple-element.618.refs_0_, f32[192,128]{1,0:T(8,128)S(1)} %collective-permute-done.50.refs_1_, f32[640,128]{1,0:T(8,128)S(1)} %get-tuple-element.617.refs_2_, ...), custom_call_target="tpu_custom_call", output_to_operand_aliasing={{0}: (4, {})} | custom-call | flops 983040 | bytes 344064 | tf_op jit(solution)/shard_map/user_log_at896/pallas_call | solution.py:484
  58.0 1.2 %collective-permute-done.49.refs_1_ = f32[192,128]{1,0:T(8,128)S(1)} collective-permute-done((f32[192,128]{1,0:T(8,128)S(1)}, f32[192,128]{1,0:T(8,128)S(1)}, u32[]{:S(2)}, u32[]{:S(2)}) %collective-permute-start.49) | collective-permute-done | bytes 98336 | tf_op jit(solution)/shard_map/ppermute | solution.py:528
  59.2 0.9 %user_log_at1088.1 = bf16[1280,128]{1,0:T(8,128)(2,1)} custom-call(f32[192,128]{1,0:T(8,128)S(1)} %get-tuple-element.616.refs_0_, f32[192,128]{1,0:T(8,128)S(1)} %collective-permute-done.49.refs_1_, f32[640,128]{1,0:T(8,128)S(1)} %get-tuple-element.617.refs_2_, f32[8,128]{1,0:T(8,128)S(1)} %get-tuple-element.628.refs_3_, ...), custom_call_target="tpu_custom_call", output_to_operand_aliasing={{}: (4, {})} | custom-call | flops 983040 | bytes 344064 | tf_op jit(solution)/shard_map/user_log_at1088/pallas_call | solution.py:484
Async XLA Ops:
  1.6 10.5 %collective-permute-start.10 = (f32[256,128]{1,0:T(8,128)S(1)}, f32[256,128]{1,0:T(8,128)S(1)}, u32[]{:S(2)}, u32[]{:S(2)}) collective-permute-start(f32[256,128]{1,0:T(8,128)S(1)} %get-tuple-element.347), channel_id=1, source_target_pairs={{0,22},{2,20},{4,18},{6,16},{8,30},{10,28},{12,26},{14,24},{16,6},... | collective-permute-start | bytes 393224 | tf_op jit(solution)/shard_map/cond/branch_10_fun/ppermute | solution.py:528
  12.9 12.7 %collective-permute-start.46 = (f32[648,128]{1,0:T(8,128)S(1)}, f32[648,128]{1,0:T(8,128)S(1)}, u32[]{:S(2)}, u32[]{:S(2)}) collective-permute-start(f32[648,128]{1,0:T(8,128)S(1)} %get-tuple-element.594.refs_1_), channel_id=1, source_target_pairs={{0,1},{1,0},{2,3},{3,2},{4,5},{5,4},{6,7},{7,6},{8,9},{9,8},{10,11... | collective-permute-start | bytes 995336 | tf_op jit(solution)/shard_map/ppermute | solution.py:528
  16.2 15.0 %collective-permute-start.45 = (f32[640,128]{1,0:T(8,128)S(1)}, f32[640,128]{1,0:T(8,128)S(1)}, u32[]{:S(2)}, u32[]{:S(2)}) collective-permute-start(f32[640,128]{1,0:T(8,128)S(1)} %get-tuple-element.592.refs_1_), channel_id=1, source_target_pairs={{0,1},{1,0},{2,3},{3,2},{4,5},{5,4},{6,7},{7,6},{8,9},{9,8},{10,11... | collective-permute-start | bytes 983048 | tf_op jit(solution)/shard_map/ppermute | solution.py:528
  16.3 9.3 %copy-start = (bf16[1280,128]{1,0:T(8,128)(2,1)S(1)}, bf16[1280,128]{1,0:T(8,128)(2,1)}, u32[]{:S(2)}) copy-start(bf16[1280,128]{1,0:T(8,128)(2,1)} %refs_3_.3) | copy-start | bytes 983044
  16.3 9.3 %collective-permute-start.22 = (f32[264,128]{1,0:T(8,128)S(1)}, f32[264,128]{1,0:T(8,128)}, u32[]{:S(2)}, u32[]{:S(2)}) collective-permute-start(f32[264,128]{1,0:T(8,128)S(1)} %get-tuple-element.433), channel_id=1, source_target_pairs={{0,16},{2,18},{4,20},{6,22},{8,24},{10,26},{12,28},{14,30},{16,0},... | collective-permute-start | bytes 405512 | tf_op jit(solution)/shard_map/cond/branch_7_fun/ppermute | solution.py:528
  27.1 14.2 %collective-permute-start.48 = (f32[648,128]{1,0:T(8,128)S(1)}, f32[648,128]{1,0:T(8,128)S(1)}, u32[]{:S(2)}, u32[]{:S(2)}) collective-permute-start(f32[648,128]{1,0:T(8,128)S(1)} %get-tuple-element.607.refs_1_), channel_id=1, source_target_pairs={{0,1},{1,0},{2,3},{3,2},{4,5},{5,4},{6,7},{7,6},{8,9},{9,8},{10,11... | collective-permute-start | bytes 995336 | tf_op jit(solution)/shard_map/ppermute | solution.py:528
  32.2 13.1 %collective-permute-start.47 = (f32[640,128]{1,0:T(8,128)S(1)}, f32[640,128]{1,0:T(8,128)S(1)}, u32[]{:S(2)}, u32[]{:S(2)}) collective-permute-start(f32[640,128]{1,0:T(8,128)S(1)} %get-tuple-element.604.refs_1_), channel_id=1, source_target_pairs={{0,1},{1,0},{2,3},{3,2},{4,5},{5,4},{6,7},{7,6},{8,9},{9,8},{10,11... | collective-permute-start | bytes 983048 | tf_op jit(solution)/shard_map/ppermute | solution.py:528
  34.3 7.0 %collective-permute-start.41 = (f32[264,128]{1,0:T(8,128)S(1)}, f32[264,128]{1,0:T(8,128)}, u32[]{:S(2)}, u32[]{:S(2)}) collective-permute-start(f32[264,128]{1,0:T(8,128)S(1)} %get-tuple-element.509), channel_id=1, source_target_pairs={{0,24},{2,26},{4,28},{6,30},{8,16},{10,18},{12,20},{14,22},{16,8},... | collective-permute-start | bytes 405512 | tf_op jit(solution)/shard_map/cond/branch_11_fun/ppermute | solution.py:528
  42.8 10.4 %collective-permute-start.53 = (f32[648,128]{1,0:T(8,128)S(1)}, f32[648,128]{1,0:T(8,128)S(1)}, u32[]{:S(2)}, u32[]{:S(2)}) collective-permute-start(f32[648,128]{1,0:T(8,128)S(1)} %get-tuple-element.621.refs_0_), channel_id=1, source_target_pairs={{0,1},{1,0},{2,3},{3,2},{4,5},{5,4},{6,7},{7,6},{8,9},{9,8},{10,11... | collective-permute-start | bytes 995336 | tf_op jit(solution)/shard_map/ppermute | solution.py:528
  46.3 9.6 %collective-permute-start.51 = (f32[264,128]{1,0:T(8,128)S(1)}, f32[264,128]{1,0:T(8,128)S(1)}, u32[]{:S(2)}, u32[]{:S(2)}) collective-permute-start(f32[264,128]{1,0:T(8,128)S(1)} %get-tuple-element.619), channel_id=1, source_target_pairs={{0,30},{2,28},{4,26},{6,24},{8,22},{10,20},{12,18},{14,16},{16,14}... | collective-permute-start | bytes 405512 | tf_op jit(solution)/shard_map/ppermute | solution.py:528
  49.7 5.3 %collective-permute-start.52 = (f32[256,128]{1,0:T(8,128)S(1)}, f32[256,128]{1,0:T(8,128)S(1)}, u32[]{:S(2)}, u32[]{:S(2)}) collective-permute-start(f32[256,128]{1,0:T(8,128)S(1)} %get-tuple-element.620.refs_0_), channel_id=1, source_target_pairs={{0,1},{1,0},{2,3},{3,2},{4,5},{5,4},{6,7},{7,6},{8,9},{9,8},{10,11... | collective-permute-start | bytes 393224 | tf_op jit(solution)/shard_map/ppermute | solution.py:528
  51.2 5.9 %collective-permute-start.50 = (f32[192,128]{1,0:T(8,128)S(1)}, f32[192,128]{1,0:T(8,128)S(1)}, u32[]{:S(2)}, u32[]{:S(2)}) collective-permute-start(f32[192,128]{1,0:T(8,128)S(1)} %get-tuple-element.618.refs_0_), channel_id=1, source_target_pairs={{0,1},{1,0},{2,3},{3,2},{4,5},{5,4},{6,7},{7,6},{8,9},{9,8},{10,11... | collective-permute-start | bytes 294920 | tf_op jit(solution)/shard_map/ppermute | solution.py:528
  51.8 7.5 %collective-permute-start.49 = (f32[192,128]{1,0:T(8,128)S(1)}, f32[192,128]{1,0:T(8,128)S(1)}, u32[]{:S(2)}, u32[]{:S(2)}) collective-permute-start(f32[192,128]{1,0:T(8,128)S(1)} %get-tuple-element.616.refs_0_), channel_id=1, source_target_pairs={{0,1},{1,0},{2,3},{3,2},{4,5},{5,4},{6,7},{7,6},{8,9},{9,8},{10,11... | collective-permute-start | bytes 294920 | tf_op jit(solution)/shard_map/ppermute | solution.py:528
